TPU v7x, 32 devices: a whole 2x2x4 slice. The times are simulated.
32 devices in a mesh: seq: 8 (over z, y), head: 4 (over x, core).
Axes of the slice: x: 2, y: 2, z: 4, core: 2. Of those that a mesh axis runs over, the one named last changes fastest.
Arguments:
- hidden_in: bfloat16 [2, 16384, 768], P(None, 'seq'), may hold values from -6 to 6
- output_cotangent: bfloat16 [2, 16384, 768], P(None, 'seq', 'head'), may hold values from -6 to 6
- input_norm_scale_gain: float32 [768], replicated, may hold values from 0.5 to 1.5
- z_proj: bfloat16 [768, 1536], P(None, 'head'), may hold values from -0.21875 to 0.21875
- x_proj: bfloat16 [768, 1536], P(None, 'head'), may hold values from -0.21875 to 0.21875
- bc_proj: bfloat16 [768, 256], replicated, may hold values from -0.21875 to 0.21875
- dt_proj: bfloat16 [768, 24], P(None, 'head'), may hold values from -0.21875 to 0.21875
- conv_x_weight: float32 [1536, 4], P('head'), may hold values from -3 to 3
- conv_x_bias: float32 [1536], P('head'), may hold values from -1.2 to 1.2
- conv_bc_weight: float32 [256, 4], replicated, may hold values from -3 to 3
- conv_bc_bias: float32 [256], replicated, may hold values from -1.2 to 1.2
- dt_bias: float32 [24], P('head'), may hold values from -2 to 0.5
- a_log: float32 [24], P('head')
- d_skip: float32 [24], P('head'), may hold values from 0.5 to 1.5
- out_norm_gain: float32 [1536], P('head'), may hold values from 0.5 to 1.5
- out_proj: bfloat16 [1536, 768], P('head'), may hold values from -0.15625 to 0.15625
- doc_starts: int32 [2, 84], replicated, may hold values from 0 to 16384, as said below
Outputs:
- layer_out: bfloat16 [2, 16384, 768], P(None, 'seq', 'head')
- input_grad: bfloat16 [2, 16384, 768], P(None, 'seq', 'head')
- grad_in_norm_gain: float32 [768], P('head')
- grad_z_proj: float32 [768, 1536], P(None, 'head')
- grad_x_proj: float32 [768, 1536], P(None, 'head')
- grad_bc_proj: float32 [768, 256], replicated
- grad_dt_proj: float32 [768, 24], P(None, 'head')
- grad_conv_x_weight: float32 [1536, 4], P('head')
- grad_conv_x_bias: float32 [1536], P('head')
- grad_conv_bc_weight: float32 [256, 4], replicated
- grad_conv_bc_bias: float32 [256], replicated
- grad_dt_bias: float32 [24], P('head')
- grad_a_log: float32 [24], P('head')
- grad_d_skip: float32 [24], P('head')
- grad_out_norm_gain: float32 [1536], P('head')
- grad_out_proj: float32 [1536, 768], P('head')
Inputs may be any that keep to these rules, and one draw needn't show every extreme that they name: doc_starts[b] holds the first positions of sequence b's documents in rising order, beginning with 0; every slot after the last document holds 16384.
All inputs are finite; a program needn't handle non-finite values.
Results may differ from a plain program's by a relative error of at most 0.0075.
The roundings to bfloat16 on the way count: a program that leaves them out, or rounds other values in their place, can miss the bound.
Values may be sent and summed in bfloat16 or wider, within the bound.
A program may use at most 256 MiB of HBM per device.

v0:
```python
import jax
import jax.numpy as jnp
from jax import lax
from jax.sharding import PartitionSpec as P

GROUP = 256


epsilon = 1e-05
highest = lax.Precision.HIGHEST


def from_behind(value, axis, steps):
    count = lax.axis_size(axis)
    leading, last = (max(0, -steps), min(count, count - steps))
    return lax.ppermute(value, axis, [(source, source + steps) for source in range(leading, last)])


def prefix(x, axis, combine, identity, reverse):
    length, index = (lax.axis_size(axis), lax.axis_index(axis))
    everything = jax.tree.map(lambda part: lax.all_gather(part, axis), x)
    start = jax.tree.map(
        lambda part, zero: jnp.broadcast_to(jnp.asarray(zero, part.dtype), part.shape), x, identity
    )

    def hop(k, before):
        at = length - 1 - k if reverse else k
        reached = at > index if reverse else at < index
        new = combine(before, jax.tree.map(lambda part: part[at], everything))
        return jax.tree.map(lambda a, b: jnp.where(reached, a, b), new, before)

    return lax.fori_loop(0, length, hop, start)


def silu_slope(inputs):
    sigma = jax.nn.sigmoid(inputs)
    return sigma * (1.0 + inputs * (1.0 - sigma))


def chain_combine(earlier, later):
    return (earlier[0] * later[0], later[0][..., None, None] * earlier[1] + later[1])


def in_blocks(array, count):
    return array.reshape((array.shape[0], count, array.shape[1] // count) + array.shape[2:])


def block_terms(seg_blocks, seg_before, delta, logdec, bmat, cmat):
    span = seg_blocks.shape[2]
    cumul = jnp.cumsum(logdec, axis=2)
    causal = jnp.arange(span)[:, None] >= jnp.arange(span)[None, :]
    inside = (seg_blocks[:, :, :, None] == seg_blocks[:, :, None, :]) & causal
    spread = cumul[:, :, :, None, :] - cumul[:, :, None, :, :]
    decay = jnp.exp(jnp.where(inside[..., None], spread, -jnp.inf))
    scores = jnp.einsum("bctn,bcsn->bcts", cmat, bmat, preferred_element_type=jnp.float32)
    product = scores[..., None] * decay * delta[:, :, None, :, :]
    ending = cumul[:, :, -1]
    tail_keep = jnp.where(
        (seg_blocks == seg_blocks[:, :, -1:])[..., None],
        jnp.exp(ending[:, :, None, :] - cumul),
        0.0,
    )
    kappa = jnp.where((seg_blocks == seg_before[:, :, None])[..., None], jnp.exp(cumul), 0.0)
    carry_keep = jnp.where((seg_blocks[:, :, -1] == seg_before)[..., None], jnp.exp(ending), 0.0)
    return (decay, scores, product, tail_keep, kappa, carry_keep)


def shards(
    hidden_in,
    output_cotangent,
    input_norm_scale_gain,
    z_proj,
    x_proj,
    bc_proj,
    dt_proj,
    conv_x_weight,
    conv_x_bias,
    conv_bc_weight,
    conv_bc_bias,
    dt_bias,
    a_log,
    d_skip,
    out_norm_gain,
    out_proj,
    doc_starts,
):
    batch, tokens, feature_width = hidden_in.shape
    inner_local = z_proj.shape[1]
    heads_local = dt_proj.shape[1]
    head_dim = inner_local // heads_local
    state_dim = bc_proj.shape[1] // 2
    taps = conv_x_weight.shape[1]
    seq_devices = lax.axis_size("seq")
    head_devices = lax.axis_size("head")
    inner_all = inner_local * head_devices
    piece_width = feature_width // head_devices
    count = tokens // GROUP
    strides = [1]
    reach = 1
    while reach < seq_devices:
        strides.append(reach)
        reach = reach * 2
    first_pos = lax.axis_index("seq") * tokens
    places = first_pos - (taps - 1) + jnp.arange(tokens + taps - 1, dtype=jnp.int32)
    seg_wide = (
        jnp.sum((doc_starts[:, None, :] <= places[None, :, None]).astype(jnp.int32), axis=-1) - 1
    )
    seg_own = seg_wide[:, taps - 1 :]
    seg_blocks = in_blocks(seg_own, count)
    seg_before = jnp.concatenate([seg_wide[:, taps - 2 : taps - 1], seg_blocks[:, :-1, -1]], axis=1)
    piece_offset = lax.axis_index("head") * piece_width
    hidden_float = hidden_in.astype(jnp.float32)
    reciprocal_root = lax.rsqrt(
        jnp.mean(hidden_float * hidden_float, axis=-1, keepdims=True) + epsilon
    )
    standardized_input = hidden_float * reciprocal_root
    normalized_rows = (standardized_input * input_norm_scale_gain).astype(jnp.bfloat16)
    gate = jnp.einsum("btd,de->bte", normalized_rows, z_proj, preferred_element_type=jnp.float32)
    conv_in = jnp.concatenate(
        [
            jnp.einsum("btd,de->bte", normalized_rows, x_proj, preferred_element_type=jnp.float32),
            jnp.einsum("btd,de->bte", normalized_rows, bc_proj, preferred_element_type=jnp.float32),
        ],
        axis=-1,
    ).astype(jnp.bfloat16)
    raw_dt = jnp.einsum("btd,de->bte", normalized_rows, dt_proj, preferred_element_type=jnp.float32)
    edge_rows = from_behind(conv_in[:, tokens - (taps - 1) :], "seq", 1)
    conv_pad = jnp.concatenate([edge_rows, conv_in], axis=1)
    conv_weight = jnp.concatenate([conv_x_weight, conv_bc_weight], axis=0)
    conv_bias = jnp.concatenate([conv_x_bias, conv_bc_bias], axis=0)
    conv_out = jnp.broadcast_to(conv_bias, conv_in.shape)
    masks = []
    for tap_index in range(taps):
        same_doc = (seg_wide[:, tap_index : tap_index + tokens] == seg_own)[..., None]
        masks.append(same_doc)
        conv_out = conv_out + jnp.where(
            same_doc,
            conv_pad[:, tap_index : tap_index + tokens].astype(jnp.float32)
            * conv_weight[:, tap_index],
            0.0,
        )
    activ = jax.nn.silu(conv_out).astype(jnp.bfloat16)
    values = in_blocks(
        activ[..., :inner_local].reshape(batch, tokens, heads_local, head_dim), count
    )
    bmat = in_blocks(activ[..., inner_local : inner_local + state_dim], count)
    cmat = in_blocks(activ[..., inner_local + state_dim :], count)
    pre_dt = raw_dt + dt_bias
    delta = in_blocks(jax.nn.softplus(pre_dt), count)
    rate = -jnp.exp(a_log)
    decay, scores, product, tail_keep, kappa, carry_keep = block_terms(
        seg_blocks, seg_before, delta, delta * rate, bmat, cmat
    )
    weights = product.astype(jnp.bfloat16)
    intra = jnp.einsum("bctsh,bcshp->bcthp", weights, values, preferred_element_type=jnp.float32)
    values_f = values.astype(jnp.float32)
    bmat_f = bmat.astype(jnp.float32)
    cmat_f = cmat.astype(jnp.float32)
    omega = tail_keep * delta
    own_state = jnp.einsum(
        "bcshp,bcsn->bchpn", values_f * omega[..., None], bmat_f, precision=highest
    )
    zero_state = jnp.zeros((batch, heads_local, head_dim, state_dim), jnp.float32)
    running = zero_state
    kept = jnp.ones((batch, heads_local), jnp.float32)
    local_in = []
    decay_before = []
    for block_index in range(count):
        local_in.append(running)
        decay_before.append(kept)
        running = carry_keep[:, block_index][..., None, None] * running + own_state[:, block_index]
        kept = kept * carry_keep[:, block_index]
    arriving = prefix(
        (kept, running), "seq", chain_combine, (jnp.ones_like(kept), zero_state), False
    )[1]
    states_in = (
        jnp.stack(local_in, axis=1)
        + jnp.stack(decay_before, axis=1)[..., None, None] * arriving[:, None]
    )
    read_rows = jnp.einsum("bctn,bchpn->bcthp", cmat_f, states_in, precision=highest)
    ssd = intra + kappa[..., None] * read_rows + d_skip[:, None] * values_f
    ssd_flat = ssd.reshape(batch, tokens, inner_local)
    gate_act = jax.nn.silu(gate)
    gated = ssd_flat * gate_act
    square_sum = lax.psum(jnp.sum(gated * gated, axis=-1), "head")
    norm_scale = lax.rsqrt(square_sum[..., None] / inner_all + epsilon)
    yhat = gated * norm_scale
    normed_out = (yhat * out_norm_gain).astype(jnp.bfloat16)
    partial_out = jnp.einsum(
        "bte,ed->btd", normed_out, out_proj, preferred_element_type=jnp.float32
    )
    out_share = lax.psum_scatter(partial_out, "head", scatter_dimension=2, tiled=True)
    own_hidden = lax.dynamic_slice_in_dim(hidden_float, piece_offset, piece_width, 2)
    layer_out = (own_hidden + out_share).astype(jnp.bfloat16)
    piece = lax.all_gather(output_cotangent, "head", axis=2, tiled=True)
    d_normed_out = jnp.einsum("btn,en->bte", piece, out_proj, preferred_element_type=jnp.float32)
    block_grad = jnp.einsum("bte,btn->en", normed_out, piece, preferred_element_type=jnp.float32)
    d_normed_out, grad_out_proj = (d_normed_out, block_grad)
    grad_out_gain = jnp.sum(d_normed_out * yhat, axis=(0, 1))
    dyhat = d_normed_out * out_norm_gain
    gate_stat = lax.psum(jnp.sum(dyhat * yhat, axis=-1), "head")
    d_gated = norm_scale * (dyhat - yhat * gate_stat[..., None] / inner_all)
    d_ssd = in_blocks(
        (d_gated * gate_act).astype(jnp.bfloat16).reshape(batch, tokens, heads_local, head_dim),
        count,
    )
    d_gate = (d_gated * ssd_flat * silu_slope(gate)).astype(jnp.bfloat16)
    d_ssd_f = d_ssd.astype(jnp.float32)
    scaled_dy = kappa[..., None] * d_ssd_f
    from_out = jnp.einsum("bcthp,bctn->bchpn", scaled_dy, cmat_f, precision=highest)
    running = zero_state
    kept = jnp.ones((batch, heads_local), jnp.float32)
    local_out = [zero_state] * count
    decay_after = [kept] * count
    for block_index in reversed(range(count)):
        local_out[block_index] = running
        decay_after[block_index] = kept
        running = carry_keep[:, block_index][..., None, None] * running + from_out[:, block_index]
        kept = kept * carry_keep[:, block_index]
    leaving = prefix(
        (kept, running), "seq", chain_combine, (jnp.ones_like(kept), zero_state), True
    )[1]
    d_states_out = (
        jnp.stack(local_out, axis=1)
        + jnp.stack(decay_after, axis=1)[..., None, None] * leaving[:, None]
    )
    grad_skip = jnp.sum(d_ssd_f * values_f, axis=(0, 1, 2, 4))
    back_rows = jnp.einsum("bcsn,bchpn->bcshp", bmat_f, d_states_out, precision=highest)
    d_values = d_skip[:, None] * d_ssd_f + omega[..., None] * back_rows
    d_omega = jnp.sum(values_f * back_rows, axis=-1)
    d_bmat = jnp.einsum(
        "bcshp,bchpn->bcsn", values_f * omega[..., None], d_states_out, precision=highest
    )
    d_kappa = jnp.sum(d_ssd_f * read_rows, axis=-1)
    d_cmat = jnp.einsum("bcthp,bchpn->bctn", scaled_dy, states_in, precision=highest)
    d_carry = jnp.sum(d_states_out * states_in, axis=(-2, -1))
    d_weights = jnp.einsum("bcthp,bcshp->bctsh", d_ssd, values, preferred_element_type=jnp.float32)
    d_values = d_values + jnp.einsum(
        "bctsh,bcthp->bcshp", weights, d_ssd, preferred_element_type=jnp.float32
    )
    d_scores = jnp.sum(d_weights * decay * delta[:, :, None, :, :], axis=-1)
    d_cmat = d_cmat + jnp.einsum("bcts,bcsn->bctn", d_scores, bmat_f, precision=highest)
    d_bmat = d_bmat + jnp.einsum("bcts,bctn->bcsn", d_scores, cmat_f, precision=highest)
    flow = d_weights * product
    omega_flow = d_omega * omega
    d_cumul = jnp.sum(flow, axis=3) - jnp.sum(flow, axis=2) + d_kappa * kappa - omega_flow
    d_cumul = d_cumul.at[:, :, -1].add(jnp.sum(omega_flow, axis=2) + d_carry * carry_keep)
    d_logdec = jnp.flip(jnp.cumsum(jnp.flip(d_cumul, 2), axis=2), 2)
    d_delta = (
        jnp.sum(d_weights * scores[..., None] * decay, axis=2)
        + d_omega * tail_keep
        + d_logdec * rate
    )
    grad_log = jnp.sum(d_logdec * delta, axis=(0, 1, 2)) * rate
    bc_grad = lax.psum(
        jnp.concatenate(
            [d_bmat.reshape(batch, tokens, state_dim), d_cmat.reshape(batch, tokens, state_dim)],
            axis=-1,
        ),
        "head",
    )
    d_conv_out = jnp.concatenate(
        [d_values.reshape(batch, tokens, inner_local), bc_grad], axis=-1
    ) * silu_slope(conv_out)
    d_pad = jnp.zeros((batch, tokens + taps - 1, conv_in.shape[2]), jnp.float32)
    weight_cols = []
    for tap_index in range(taps):
        masked = jnp.where(masks[tap_index], d_conv_out, 0.0)
        d_pad = d_pad.at[:, tap_index : tap_index + tokens].add(masked * conv_weight[:, tap_index])
        weight_cols.append(
            jnp.sum(
                masked * conv_pad[:, tap_index : tap_index + tokens].astype(jnp.float32),
                axis=(0, 1),
            )
        )
    grad_conv_weight = jnp.stack(weight_cols, axis=1)
    grad_conv_bias = jnp.sum(d_conv_out, axis=(0, 1))
    returned = from_behind(d_pad[:, : taps - 1], "seq", -1)
    d_conv_in = d_pad[:, taps - 1 :].at[:, tokens - (taps - 1) :].add(returned).astype(jnp.bfloat16)
    d_raw_f = d_delta.reshape(batch, tokens, heads_local) * jax.nn.sigmoid(pre_dt)
    grad_dt_bias = jnp.sum(d_raw_f, axis=(0, 1))
    d_raw = d_raw_f.astype(jnp.bfloat16)
    d_conv_x = d_conv_in[..., :inner_local]
    d_conv_bc = d_conv_in[..., inner_local:]
    grad_z = jnp.einsum("btd,bte->de", normalized_rows, d_gate, preferred_element_type=jnp.float32)
    grad_x = jnp.einsum(
        "btd,bte->de", normalized_rows, d_conv_x, preferred_element_type=jnp.float32
    )
    grad_bc = jnp.einsum(
        "btd,bte->de", normalized_rows, d_conv_bc, preferred_element_type=jnp.float32
    )
    grad_dt = jnp.einsum("btd,bte->de", normalized_rows, d_raw, preferred_element_type=jnp.float32)
    partial_in = jnp.einsum("bte,de->btd", d_gate, z_proj, preferred_element_type=jnp.float32)
    partial_in = partial_in + jnp.einsum(
        "bte,de->btd", d_conv_x, x_proj, preferred_element_type=jnp.float32
    )
    partial_in = partial_in + jnp.einsum(
        "bte,de->btd", d_raw, dt_proj, preferred_element_type=jnp.float32
    )
    normalized_grad = lax.psum_scatter(partial_in, "head", scatter_dimension=2, tiled=True)
    bc_rows = lax.dynamic_slice_in_dim(bc_proj, piece_offset, piece_width, 0)
    normalized_grad = normalized_grad + jnp.einsum(
        "btc,ec->bte", d_conv_bc, bc_rows, preferred_element_type=jnp.float32
    )
    local_standardized = lax.dynamic_slice_in_dim(standardized_input, piece_offset, piece_width, 2)
    local_gain_slice = lax.dynamic_slice_in_dim(input_norm_scale_gain, piece_offset, piece_width, 0)
    input_gain_gradient = jnp.sum(normalized_grad * local_standardized, axis=(0, 1))
    standardized_grad = normalized_grad * local_gain_slice
    input_statistics = lax.psum(jnp.sum(standardized_grad * local_standardized, axis=-1), "head")
    input_grad = (
        output_cotangent.astype(jnp.float32)
        + reciprocal_root
        * (standardized_grad - local_standardized * input_statistics[..., None] / feature_width)
    ).astype(jnp.bfloat16)
    summed = lax.psum(
        (
            input_gain_gradient,
            grad_z,
            grad_x,
            grad_bc,
            grad_dt,
            grad_conv_weight[:inner_local],
            grad_conv_bias[:inner_local],
            grad_conv_weight[inner_local:],
            grad_conv_bias[inner_local:],
            grad_dt_bias,
            grad_log,
            grad_skip,
            grad_out_gain,
            grad_out_proj,
        ),
        "seq",
    )
    return (layer_out, input_grad) + tuple(summed)


def solution(mesh):
    return jax.shard_map(
        shards,
        mesh=mesh,
        in_specs=(
            P(None, "seq", None),
            P(None, "seq", "head"),
            P(),
            P(None, "head"),
            P(None, "head"),
            P(),
            P(None, "head"),
            P("head", None),
            P("head"),
            P(),
            P(),
            P("head"),
            P("head"),
            P("head"),
            P("head"),
            P("head", None),
            P(),
        ),
        out_specs=(
            P(None, "seq", "head"),
            P(None, "seq", "head"),
            P("head"),
            P(None, "head"),
            P(None, "head"),
            P(),
            P(None, "head"),
            P("head", None),
            P("head"),
            P(),
            P(),
            P("head"),
            P("head"),
            P("head"),
            P("head"),
            P("head", None),
        ),
        check_vma=False,
    )
```

profile of v0, /device:TPU:0, one launch (start us, length us, event | category | flops | bytes accessed | tf_op | source)
XLA Modules:
  0.0 983.6 jit_solution(16018611316426339155)
XLA Ops:
  7.2 8.7 copy.749
  20.4 12.6 %broadcast_multiply_fusion = (f32[2,2048,768]{1,2,0:T(8,128)}, bf16[2,2048,768]{1,2,0:T(8,128)(2,1)}) fusion(f32[2,2048]{1,0:T(2,128)S(1)} %add_rsqrt_fusion.1, bf16[2,2048,768]{1,2,0:T(8,128)(2,1)} %copy.749, f32[768]{0:T(1024)S(1)} %copy-done.118), kind=kLoop, calls=%fused_computation.75 | loop fusion | flops 12582912 | bytes 25185280 | tf_op jit(solution)/shard_map/mul | solution.py:116
  43.4 6.2 collective-permute-start
  63.1 6.8 reduce-window.14
  76.0 5.2 exponential_select_fusion.1
  88.8 13.2 %multiply_convert_fusion.1 = (bf16[2,2048,640]{1,2,0:T(8,128)(2,1)S(1)}, f32[2,2048,640]{1,2,0:T(8,128)}) fusion(f32[640]{0:T(1024)S(1)} %get-tuple-element.366, bf16[2,2048,256]{1,2,0:T(8,128)(2,1)S(1)} %convolution_convert_fusion.1, bf16[2,2048,384]{1,2,0:T(8,128)(2,1)S(1)} %copy-done.6, f32[640]{0:T(1024)S(1)} %get-tuple-element.367, ...), kind=kLoop, calls=%fused_computation.44 | loop fusion | flops 60293120 | bytes 36725248 | tf_op jit(solution)/shard_map/convert_element_type | solution.py:142
  125.2 18.1 %all_gather.19 = f32[8,2,6]{2,1,0:T(2,128)S(1)} all-gather(f32[1,2,6]{2,1,0:T(2,128)S(1)} %get-tuple-element.460), channel_id=1, replica_groups=mesh['seq'=8,'head'=4] {'seq'}, dimensions={0}, use_global_device_ids=true | all-gather | bytes 432 | tf_op jit(solution)/shard_map/all_gather | solution.py:21
  163.0 15.3 %all-gather.4.cloned.1.call-done = f32[8,2,6,64,128]{4,3,2,1,0:T(8,128)} async-done(((f32[1,2,6,64,128]{4,3,2,1,0:T(8,128)}), f32[8,2,6,64,128]{4,3,2,1,0:T(8,128)}) %all-gather.4.cloned.1.call-update) | async-done | bytes 3145744 | tf_op jit(solution)/shard_map/all_gather | solution.py:21
  178.3 9.5 while.36
  187.9 5.5 fusion.41
  193.5 8.7 fusion.26
  202.2 7.5 copy.806
  209.7 7.2 reshape.699
  216.8 13.4 %multiply_reduce_fusion.4 = (f32[2,2048]{1,0:T(2,128)S(1)}, f32[2,2048,384]{1,2,0:T(8,128)}, f32[2,2048,384]{1,2,0:T(8,128)}) fusion(f32[2,2048,384]{1,2,0:T(8,128)} %reshape.699, bf16[2,2048,768]{1,2,0:T(8,128)(2,1)} %get-tuple-element.438, bf16[768,384]{1,0:T(8,128)(2,1)S(1)} %copy-done), kind=kOutput, calls=%fused_computation.72 | convolution fusion | flops 2426925056 | bytes 25772032 | tf_op jit(solution)/shard_map/btd,de->bte/dot_general | solution.py:118
  230.2 10.1 %psum.126 = f32[2,2048]{1,0:T(2,128)S(1)} all-reduce(f32[2,2048]{1,0:T(2,128)S(1)} %get-tuple-element.420), channel_id=1, replica_groups=mesh['seq'=8,'head'=4] {'head'}, use_global_device_ids=true, to_apply=%region_7.8 | all-reduce | flops 4096 | bytes 32768 | tf_op jit(solution)/shard_map/psum | solution.py:185
  240.4 11.0 %multiply_reduce_fusion.1 = (f32[384]{0:T(512)}, f32[2,2048]{1,0:T(2,128)S(1)}, f32[2,2048,384]{1,2,0:T(8,128)}) fusion(f32[2,2048,384]{1,2,0:T(8,128)} %get-tuple-element.421, f32[2,2048]{1,0:T(2,128)S(1)} %add_rsqrt_fusion, f32[384]{0:T(512)S(1)} %copy-done.111, bf16[2,2048,768]{1,2,0:T(8,128)(2,1)} %all-gather.6.cloned.1.call-done, ...), kind=kOutput, calls=%fused_computation.65 | convolution fusion | flops 2425351680 | bytes 19500032 | tf_op jit(solution)/shard_map/btn,en->bte/dot_general | solution.py:196
  251.4 10.3 %psum.127 = f32[2,2048]{1,0:T(2,128)S(1)} all-reduce(f32[2,2048]{1,0:T(2,128)S(1)} %get-tuple-element.362), channel_id=1, replica_groups=mesh['seq'=8,'head'=4] {'head'}, use_global_device_ids=true, to_apply=%region_10.11 | all-reduce | flops 4096 | bytes 32768 | tf_op jit(solution)/shard_map/psum | solution.py:201
  261.7 14.8 %multiply_reduce_fusion.2 = (f32[384]{0:T(512)}, bf16[2,2048,384]{1,2,0:T(8,128)(2,1)S(1)}, bf16[2,2048,384]{1,2,0:T(8,128)(2,1)}) fusion(bf16[2,2048,640]{1,2,0:T(8,128)(2,1)} %copy-done.7, f32[2,2048,384]{1,2,0:T(8,128)} %get-tuple-element.477, f32[2,2048]{1,0:T(2,128)S(1)} %psum.127, f32[2,2048,384]{1,2,0:T(8,128)} %get-tuple-element.421, ...), kind=kLoop, calls=%fused_computation.66 | loop fusion | flops 36175488 | bytes 34638848 | tf_op jit(solution)/shard_map/reduce_sum | solution.py:227
  287.2 20.4 %all_gather.22 = f32[8,2,6]{2,1,0:T(2,128)} all-gather(f32[1,2,6]{2,1,0:T(2,128)S(1)} %copy-done.122), channel_id=1, replica_groups=mesh['seq'=8,'head'=4] {'seq'}, dimensions={0}, use_global_device_ids=true | all-gather | bytes 432 | tf_op jit(solution)/shard_map/all_gather | solution.py:21
  307.6 22.5 %fusion.7 = (f32[2,8,256,6]{2,3,1,0:T(8,128)}, f32[2,8,256,6]{2,3,1,0:T(8,128)}, f32[2,8,256,6]{2,3,1,0:T(8,128)}, f32[2,8,256,256]{3,2,1,0:T(8,128)S(1)}) fusion(f32[2,8,256,6]{2,3,1,0:T(8,128)S(1)} %bitcast.429, f32[2,8,256,6]{2,3,1,0:T(8,128)} %copy-done.64, f32[2,8,256,256]{3,2,1,0:T(8,128)} %fusion.134, pred[2,8,256,256]{3,2,1,0:T(8,128)(4,1)} %compare_and_fusion, ...), kind=kOutput, calls=%fused_computation.16 | convolution fusion | flops 885972992 | bytes 16220160 | tf_op jit(solution)/shard_map/bcthp,bcshp->bctsh/dot_general | solution.py:237
  334.5 12.3 %bitcast_add_fusion.3 = f32[2,8,256,128]{3,2,1,0:T(8,128)} fusion(f32[2,8,256,128]{3,2,1,0:T(8,128)S(1)} %fusion.135, f32[2,8,256,6]{2,3,1,0:T(8,128)S(1)} %copy.772, bf16[2,8,256,6,64]{2,1,4,3,0:T(8,128)(2,1)S(1)} %bitcast.404, f32[2,8,6,64,128]{4,3,2,0,1:T(8,128)S(1)} %copy-done.12, f32[2,6,64,128]{3,2,1,0:T(8,128)S(1)} %get-tuple-element.314, ...), kind=kOutput, calls=%fused_computation.107 | convolution fusion | flops 2421161984 | bytes 10977664 | tf_op jit(solution)/shard_map/bcthp,bchpn->bctn/dot_general | solution.py:235
  361.2 14.3 %while.37 = (s32[]{:T(128)}, f32[2,6,64,128]{3,2,1,0:T(8,128)S(1)}, s32[]{:T(128)}, f32[8,2,6]{2,1,0:T(2,128)}, f32[8,2,6,64,128]{4,3,2,1,0:T(8,128)}, /*index=5*/s32[]{:T(128)}, s32[]{:T(128)}, s32[]{:T(128)}, s32[]{:T(128)}) while((s32[]{:T(128)}, f32[2,6,64,128]{3,2,1,0:T(8,128)S(1)}, s32[]{:T(128)}, f32[8,2,6]{2,1,0:T(2,128)}, ...), condition=%wide.region_12.13_spmd.clone, body=%wide.region_11.12_spmd.clone.sunk | while | flops 393224 | bytes 1179967 | solution.py:32
  380.1 10.9 %fusion.24 = f32[2,8,256,128,1]{3,2,4,1,0:T(8,128)S(1)} fusion(f32[2,8,256,6]{2,3,1,0:T(8,128)S(1)} %copy.779, f32[2,8,6,64,128]{4,3,2,0,1:T(8,128)S(1)} %get-tuple-element.409, bf16[2,8,256,6,64]{2,1,4,3,0:T(8,128)(2,1)S(1)} %bitcast.400), kind=kOutput, calls=%fused_computation.55 | convolution fusion | flops 2419064832 | bytes 8486912 | tf_op jit(solution)/shard_map/bcshp,bchpn->bcsn/dot_general | solution.py:231
  403.0 10.2 %fusion.75 = f32[2,2048,768]{1,2,0:T(8,128)} fusion(bf16[384,768]{1,0:T(8,128)(2,1)S(1)} %copy-done.48, f32[2,2048,384]{1,2,0:T(8,128)} %get-tuple-element.421, f32[384]{0:T(512)} %param.47, f32[2,2048]{1,0:T(2,128)S(1)} %add_rsqrt_fusion), kind=kOutput, calls=%fused_computation.137 | convolution fusion | flops 2420637696 | bytes 19482112 | tf_op jit(solution)/shard_map/bte,ed->btd/dot_general | solution.py:189
  417.9 8.9 fusion.77
  430.5 8.9 fusion.29
  439.4 7.0 copy.829
  446.4 7.4 reshape.700
  455.4 7.8 multiply_reduce_fusion.9
  470.2 6.8 reduce-window.16
  490.3 23.9 %fusion.14 = (f32[640]{0:T(1024)S(1)}, f32[640]{0:T(1024)S(1)}, f32[640]{0:T(1024)S(1)}, f32[640]{0:T(1024)S(1)}, f32[640]{0:T(1024)S(1)}, /*index=5*/f32[2,2048,640]{1,2,0:T(8,128)S(1)}) fusion(pred[2,2048]{1,0:T(4,128)(4,1)S(1)} %copy-done.62, bf16[2,2051,640]{1,2,0:T(8,128)(2,1)} %copy-done.3, pred[2,2048]{1,0:T(4,128)(4,1)S(1)} %copy-done.60, ...), kind=kLoop, calls=%fused_computation.34 | loop fusion | flops 73397120 | bytes 52453888 | tf_op jit(solution)/shard_map/reduce_sum | solution.py:271
  514.2 6.8 select_multiply_fusion
  521.0 10.0 %scatter-add.16 = f32[2,2051,640]{1,2,0:T(8,128)} pad(f32[2,2048,640]{1,2,0:T(8,128)} %select_multiply_fusion, f32[]{:T(128)} %constant.276.clone.1), padding=0_0x0_3x0_0 | pad | bytes 20986884 | tf_op jit(solution)/shard_map/scatter-add | solution.py:269
  531.1 10.6 %multiply_add_fusion = f32[2,2048,640]{1,2,0:T(8,128)} fusion(f32[2,2048,640]{1,2,0:T(8,128)S(1)} %get-tuple-element.407, f32[640]{0:T(1024)S(1)} %copy-done.96, pred[2,2048]{1,0:T(4,128)(4,1)S(1)} %copy-done.60, f32[2,2048,640]{1,2,0:T(8,128)} %select_multiply_fusion), kind=kLoop, calls=%fused_computation.43 | loop fusion | flops 7864320 | bytes 31463936 | tf_op jit(solution)/shard_map/add | solution.py:269
  541.6 54.3 %scatter-add.19 = f32[2,2051,640]{1,2,0:T(8,128)} dynamic-update-slice(f32[2,2051,640]{1,2,0:T(8,128)} %scatter-add.16, f32[2,2048,640]{1,2,0:T(8,128)} %multiply_add_fusion, s32[]{:T(128)} %constant.267.clone.1, s32[]{:T(128)} %constant.282.clone.1, s32[]{:T(128)} %constant.267.clone.1) | dynamic-update-slice | bytes 20971524 | tf_op jit(solution)/shard_map/scatter-add | solution.py:269
  595.9 12.9 %slice_add_fusion.1 = f32[2,2048,640]{1,2,0:T(8,128)} fusion(f32[2,2051,640]{1,2,0:T(8,128)} %scatter-add.19, f32[2,2048,640]{1,2,0:T(8,128)} %copy-done.2, f32[640]{0:T(1024)S(1)} %copy-done.94, pred[2,2048]{1,0:T(4,128)(4,1)S(1)} %copy-done.58), kind=kLoop, calls=%fused_computation.41 | loop fusion | flops 7864320 | bytes 31463936 | tf_op jit(solution)/shard_map/add | solution.py:269
  608.8 54.0 %scatter-add.20 = f32[2,2051,640]{1,2,0:T(8,128)} dynamic-update-slice(f32[2,2051,640]{1,2,0:T(8,128)} %scatter-add.19, f32[2,2048,640]{1,2,0:T(8,128)} %slice_add_fusion.1, s32[]{:T(128)} %constant.267.clone.1, s32[]{:T(128)} %constant.283.clone.1, s32[]{:T(128)} %constant.267.clone.1) | dynamic-update-slice | bytes 20971524 | tf_op jit(solution)/shard_map/scatter-add | solution.py:269
  665.4 12.8 %slice_add_fusion = f32[2,2048,640]{1,2,0:T(8,128)} fusion(f32[2,2051,640]{1,2,0:T(8,128)} %scatter-add.20, f32[2,2048,640]{1,2,0:T(8,128)} %copy-done.2, f32[640]{0:T(1024)S(1)} %copy-done.92), kind=kLoop, calls=%fused_computation.40 | loop fusion | flops 5242880 | bytes 31459840 | tf_op jit(solution)/shard_map/add | solution.py:269
  679.9 5.8 scatter-add.21
  694.1 11.1 %add_add_fusion = f32[2,2048,768]{1,2,0:T(8,128)} fusion(f32[2,2048,768]{1,2,0:T(8,128)} %fusion.77, f32[2,2048,768]{1,2,0:T(8,128)S(1)} %fusion.45, bf16[2,2048,6]{1,2,0:T(8,128)(2,1)S(1)} %get-tuple-element.406, bf16[768,6]{0,1:T(8,128)(2,1)S(1)} %copy-done.87), kind=kOutput, calls=%fused_computation.26 | convolution fusion | flops 44040192 | bytes 37807104 | tf_op jit(solution)/shard_map/bte,de->btd/dot_general | solution.py:297
  705.5 8.5 convolution_bitcast_fusion.1
  714.0 11.3 %convolution_bitcast_fusion = f32[384,768]{1,0:T(8,128)} fusion(bf16[2,2048,768]{1,2,0:T(8,128)(2,1)} %all-gather.6.cloned.1.call-done, f32[2,2048,384]{1,2,0:T(8,128)} %get-tuple-element.421, f32[384]{0:T(512)S(1)} %copy-done.112, f32[2,2048]{1,0:T(2,128)S(1)} %add_rsqrt_fusion), kind=kOutput, calls=%fused_computation.126 | convolution fusion | flops 2420637696 | bytes 13780480 | tf_op jit(solution)/shard_map/bte,btn->en/dot_general | solution.py:197
  732.6 9.0 convert_element_type.70
  752.0 50.8 %reduce-scatter.5.cloned.1.call-done = f32[2,2048,192]{1,2,0:T(8,128)} async-done(((f32[2,2048,768]{1,2,0:T(8,128)}), f32[2,2048,192]{1,2,0:T(8,128)}) %reduce-scatter.5.cloned.1.call-update) | async-done | bytes 3145744 | tf_op jit(solution)/shard_map/reduce_scatter | solution.py:300
  802.8 6.2 multiply_reduce_fusion.5
  809.1 40.6 %all-reduce.1 = (f32[192]{0:T(256)}, f32[768,6]{0,1:T(8,128)}, f32[384,4]{0,1:T(4,128)}, f32[384]{0:T(512)}, f32[256,4]{0,1:T(4,128)}, /*index=5*/f32[256]{0:T(2...) all-reduce(f32[192]{0:T(256)S(1)} %get-tuple-element.359, ...), channel_id=1, replica_groups=mesh['seq'=8,'head'=4] {'seq'}, use_global_device_ids=true, to_apply=%region_28.29 | all-reduce | flops 8402 | bytes 67216 | tf_op jit(solution)/shard_map/psum | solution.py:315
  849.7 10.9 %psum.129 = f32[2,2048]{1,0:T(2,128)S(1)} all-reduce(f32[2,2048]{1,0:T(2,128)S(1)} %get-tuple-element.360), channel_id=1, replica_groups=mesh['seq'=8,'head'=4] {'head'}, use_global_device_ids=true, to_apply=%region_26.27 | all-reduce | flops 4096 | bytes 32768 | tf_op jit(solution)/shard_map/psum | solution.py:309
  865.8 104.1 %all-reduce.8.cloned.1.call-done = (f32[768,384]{1,0:T(8,128)}, f32[768,384]{1,0:T(8,128)}, f32[768,256]{1,0:T(8,128)}, f32[384,768]{1,0:T(8,128)}) async-done(((f32[768,384]{1,0:T(8,128)}, f32[768,384]{1,0:T(8,128)}, f32[768,256]{1,0:T(8,128)}, f32[384,768]{1,0:T(8,128)}), (f32[768,384]{1,0:T(8,128)}, f32[768,384]{1,0:T(8,128)}, f32[768,256]{1,0:T(8,128)}, ...) | async-done | bytes 4325392 | tf_op jit(solution)/shard_map/psum | solution.py:315
  (491 shorter events, 225.4 us)
Async XLA Ops:
  7.2 209.7 %copy-start = (bf16[768,384]{1,0:T(8,128)(2,1)S(1)}, bf16[768,384]{1,0:T(8,128)(2,1)}, u32[]{:S(2)}) copy-start(bf16[768,384]{1,0:T(8,128)(2,1)} %param.36) | copy-start | bytes 1769476
  7.2 171.1 %all-gather.4.cloned.1.call-start = ((), (), s32[]{:S(2)}) async-start(), calls=%async_computation.2 | async-start | bytes 3538944 | tf_op jit(solution)/shard_map/all_gather | solution.py:21
  37.9 50.8 %copy-start.8 = (bf16[2,2048,256]{1,2,0:T(8,128)(2,1)}, bf16[2,2048,256]{1,2,0:T(8,128)(2,1)S(1)}, u32[]{:S(2)}) copy-start(bf16[2,2048,256]{1,2,0:T(8,128)(2,1)S(1)} %convolution_convert_fusion.1) | copy-start | bytes 6291460
  43.4 40.2 %collective-permute-start = (bf16[2,3,640]{1,2,0:T(8,128)(2,1)}, bf16[2,3,640]{1,2,0:T(8,128)(2,1)}, u32[]{:S(2)}, u32[]{:S(2)}) collective-permute-start(bf16[2,3,640]{1,2,0:T(8,128)(2,1)} %fusion.105), channel_id=1, source_target_pairs={{0,4},{4,8},{8,12},{12,16},{16,20},{20,24},{24,28},{1,5},{5,9},{9,... | collective-permute-start | bytes 23048 | tf_op jit(solution)/shard_map/ppermute | solution.py:16
  50.7 38.0 %copy-start.57 = (pred[2,2048]{1,0:T(4,128)(4,1)}, pred[2,2048]{1,0:T(4,128)(4,1)S(1)}, u32[]{:S(2)}) copy-start(pred[2,2048]{1,0:T(4,128)(4,1)S(1)} %get-tuple-element.457) | copy-start | bytes 12292
  50.7 38.0 %copy-start.59 = (pred[2,2048]{1,0:T(4,128)(4,1)}, pred[2,2048]{1,0:T(4,128)(4,1)S(1)}, u32[]{:S(2)}) copy-start(pred[2,2048]{1,0:T(4,128)(4,1)S(1)} %get-tuple-element.458) | copy-start | bytes 12292
  50.7 38.0 %copy-start.61 = (pred[2,2048]{1,0:T(4,128)(4,1)}, pred[2,2048]{1,0:T(4,128)(4,1)S(1)}, u32[]{:S(2)}) copy-start(pred[2,2048]{1,0:T(4,128)(4,1)S(1)} %get-tuple-element.456) | copy-start | bytes 12292
  55.5 138.0 %copy-start.50 = (f32[2,2048,6]{1,2,0:T(8,128)}, f32[2,2048,6]{1,2,0:T(8,128)S(1)}, u32[]{:S(2)}) copy-start(f32[2,2048,6]{1,2,0:T(8,128)S(1)} %get-tuple-element.475) | copy-start | bytes 294916
  55.5 19.3 %copy-start.119 = (f32[384,4]{0,1:T(4,128)S(1)}, f32[384,4]{0,1:T(4,128)}, u32[]{:S(2)}) copy-start(f32[384,4]{0,1:T(4,128)} %param.40) | copy-start | bytes 18436
  55.5 19.3 %copy-start.123 = (f32[256,4]{0,1:T(4,128)S(1)}, f32[256,4]{0,1:T(4,128)}, u32[]{:S(2)}) copy-start(f32[256,4]{0,1:T(4,128)} %param.42) | copy-start | bytes 12292
  63.1 18.0 %copy-start.125 = (f32[384]{0:T(512)S(1)}, f32[384]{0:T(512)}, u32[]{:S(2)}) copy-start(f32[384]{0:T(512)} %param.41) | copy-start | bytes 4612
  63.1 18.0 %copy-start.130 = (f32[256]{0:T(256)S(1)}, f32[256]{0:T(256)}, u32[]{:S(2)}) copy-start(f32[256]{0:T(256)} %param.43) | copy-start | bytes 3076
  74.9 44.0 %copy-start.115 = (f32[2,1,6]{2,0,1:T(2,128)}, f32[2,1,6]{2,0,1:T(2,128)S(1)}, u32[]{:S(2)}) copy-start(f32[2,1,6]{2,0,1:T(2,128)S(1)} %copy.775) | copy-start | bytes 148
  83.0 68.8 %copy-start.88 = (f32[2,1,6]{2,0,1:T(2,128)}, f32[2,1,6]{2,0,1:T(2,128)S(1)}, u32[]{:S(2)}) copy-start(f32[2,1,6]{2,0,1:T(2,128)S(1)} %copy.782) | copy-start | bytes 148
  83.1 72.6 %copy-start.80 = (f32[2,1,6]{2,0,1:T(2,128)}, f32[2,1,6]{2,0,1:T(2,128)S(1)}, u32[]{:S(2)}) copy-start(f32[2,1,6]{2,0,1:T(2,128)S(1)} %copy.784) | copy-start | bytes 148
  83.2 72.5 %copy-start.77 = (f32[2,1,6]{2,0,1:T(2,128)}, f32[2,1,6]{2,0,1:T(2,128)S(1)}, u32[]{:S(2)}) copy-start(f32[2,1,6]{2,0,1:T(2,128)S(1)} %copy.786) | copy-start | bytes 148
  83.3 75.3 %copy-start.83 = (f32[2,1,6]{2,0,1:T(2,128)}, f32[2,1,6]{2,0,1:T(2,128)S(1)}, u32[]{:S(2)}) copy-start(f32[2,1,6]{2,0,1:T(2,128)S(1)} %copy.788) | copy-start | bytes 148
  83.4 75.2 %copy-start.74 = (f32[2,1,6]{2,0,1:T(2,128)}, f32[2,1,6]{2,0,1:T(2,128)S(1)}, u32[]{:S(2)}) copy-start(f32[2,1,6]{2,0,1:T(2,128)S(1)} %copy.790) | copy-start | bytes 148
  83.5 76.0 %copy-start.97 = (f32[2,1,6]{2,0,1:T(2,128)}, f32[2,1,6]{2,0,1:T(2,128)S(1)}, u32[]{:S(2)}) copy-start(f32[2,1,6]{2,0,1:T(2,128)S(1)} %copy.792) | copy-start | bytes 148
  118.1 122.3 %all-gather.6.cloned.1.call-start = ((), (), s32[]{:S(2)}) async-start(), calls=%async_computation.4 | async-start | bytes 7864320 | tf_op jit(solution)/shard_map/all_gather | solution.py:195
  118.8 242.4 %all-gather.8.cloned.1.call-start = ((), (), s32[]{:S(2)}) async-start(), calls=%async_computation.5 | async-start | bytes 3538944 | tf_op jit(solution)/shard_map/all_gather | solution.py:21
  123.2 70.3 %copy-start.64 = (f32[2,8,256,6]{2,3,1,0:T(8,128)}, f32[2,8,256,6]{2,3,1,0:T(8,128)S(1)}, u32[]{:S(2)}) copy-start(f32[2,8,256,6]{2,3,1,0:T(8,128)S(1)} %copy.766) | copy-start | bytes 294916
  123.2 32.4 %copy-start.72 = (f32[2,1,6]{1,0,2:T(2,128)}, f32[2,1,6]{1,0,2:T(2,128)S(1)}, u32[]{:S(2)}) copy-start(f32[2,1,6]{1,0,2:T(2,128)S(1)} %broadcast.365) | copy-start | bytes 148
  123.4 64.4 %copy-start.53 = (f32[2,8,6]{2,0,1:T(2,128)}, f32[2,8,6]{2,0,1:T(2,128)S(1)}, u32[]{:S(2)}) copy-start(f32[2,8,6]{2,0,1:T(2,128)S(1)} %copy.794) | copy-start | bytes 1156
  216.8 23.6 %copy-start.48 = (bf16[384,768]{1,0:T(8,128)(2,1)S(1)}, bf16[384,768]{1,0:T(8,128)(2,1)}, u32[]{:S(2)}) copy-start(bf16[384,768]{1,0:T(8,128)(2,1)} %param.48) | copy-start | bytes 1769476
  216.8 23.6 %copy-start.111 = (f32[384]{0:T(512)S(1)}, f32[384]{0:T(512)}, u32[]{:S(2)}) copy-start(f32[384]{0:T(512)} %param.47) | copy-start | bytes 4612
  280.1 27.5 %copy-start.51 = (f32[2,2048,6]{1,2,0:T(8,128)S(1)}, f32[2,2048,6]{1,2,0:T(8,128)}, u32[]{:S(2)}) copy-start(f32[2,2048,6]{1,2,0:T(8,128)} %copy-done.50) | copy-start | bytes 294916
  286.2 204.1 %all-reduce.6.cloned.1.call-start = ((), (), s32[]{:S(2)}) async-start(), calls=%async_computation.6 | async-start | bytes 8388608 | tf_op jit(solution)/shard_map/psum | solution.py:255
  307.6 22.5 %copy-start.32 = (bf16[2,8,256,128]{3,2,1,0:T(8,128)(2,1)S(1)}, bf16[2,8,256,128]{3,2,1,0:T(8,128)(2,1)}, u32[]{:S(2)}) copy-start(bf16[2,8,256,128]{3,2,1,0:T(8,128)(2,1)} %copy.756) | copy-start | bytes 3145732
  330.1 16.7 %copy-start.25 = (f32[2,8,256,256]{3,2,1,0:T(8,128)}, f32[2,8,256,256]{3,2,1,0:T(8,128)S(1)}, u32[]{:S(2)}) copy-start(f32[2,8,256,256]{3,2,1,0:T(8,128)S(1)} %get-tuple-element.355) | copy-start | bytes 12582916
  355.2 20.3 %copy-start.102 = (f32[2,8,6]{2,0,1:T(2,128)S(1)}, f32[2,8,6]{2,0,1:T(2,128)}, u32[]{:S(2)}) copy-start(f32[2,8,6]{2,0,1:T(2,128)} %copy.824) | copy-start | bytes 1156
  380.1 16.0 %copy-start.27 = (f32[2,8,6,64,128]{4,3,2,0,1:T(8,128)}, f32[2,8,6,64,128]{4,3,2,0,1:T(8,128)S(1)}, u32[]{:S(2)}) copy-start(f32[2,8,6,64,128]{4,3,2,0,1:T(8,128)S(1)} %get-tuple-element.409) | copy-start | bytes 9437188
  403.0 344.6 %reduce-scatter.3.cloned.1.call-start = ((), (), s32[]{:S(2)}) async-start(), calls=%async_computation.3 | async-start | bytes 15728640 | tf_op jit(solution)/shard_map/reduce_scatter | solution.py:192
  413.3 389.5 %reduce-scatter.5.cloned.1.call-start = ((), (), s32[]{:S(2)}) async-start(), calls=%async_computation.7 | async-start | bytes 15728640 | tf_op jit(solution)/shard_map/reduce_scatter | solution.py:300
  463.2 18.1 %copy-start.63 = (f32[2,8,256,6]{2,3,1,0:T(8,128)S(1)}, f32[2,8,256,6]{2,3,1,0:T(8,128)}, u32[]{:S(2)}) copy-start(f32[2,8,256,6]{2,3,1,0:T(8,128)} %get-tuple-element.354) | copy-start | bytes 294916
  464.6 18.3 %copy-start.23 = (f32[2,8,256,6]{1,0,3,2:T(2,128)S(1)}, f32[2,8,256,6]{1,0,3,2:T(2,128)}, u32[]{:S(2)}) copy-start(f32[2,8,256,6]{1,0,3,2:T(2,128)} %copy.759) | copy-start | bytes 294916
  464.6 18.3 %copy-start.128 = (f32[6]{0:T(128)S(1)}, f32[6]{0:T(128)}, u32[]{:S(2)}) copy-start(f32[6]{0:T(128)} %copy-done.127) | copy-start | bytes 76
  490.3 23.9 %copy-start.101 = (f32[640]{0:T(1024)S(1)}, f32[640]{0:T(1024)}, u32[]{:S(2)}) copy-start(f32[640]{0:T(1024)} %copy-done.100) | copy-start | bytes 7684
  514.2 16.8 %copy-start.2 = (f32[2,2048,640]{1,2,0:T(8,128)}, f32[2,2048,640]{1,2,0:T(8,128)S(1)}, u32[]{:S(2)}) copy-start(f32[2,2048,640]{1,2,0:T(8,128)S(1)} %get-tuple-element.407) | copy-start | bytes 31457284
  541.6 54.3 %copy-start.94 = (f32[640]{0:T(1024)S(1)}, f32[640]{0:T(1024)}, u32[]{:S(2)}) copy-start(f32[640]{0:T(1024)} %copy-done.93) | copy-start | bytes 7684
  608.8 56.6 %copy-start.92 = (f32[640]{0:T(1024)S(1)}, f32[640]{0:T(1024)}, u32[]{:S(2)}) copy-start(f32[640]{0:T(1024)} %copy-done.91) | copy-start | bytes 7684
  664.1 14.2 %collective-permute-start.1 = (f32[2,3,640]{2,0,1:T(2,128)S(1)}, f32[2,3,640]{2,0,1:T(2,128)S(1)}, u32[]{:S(2)}, u32[]{:S(2)}) collective-permute-start(f32[2,3,640]{2,0,1:T(2,128)S(1)} %copy.839), channel_id=1, source_target_pairs={{4,0},{8,4},{12,8},{16,12},{20,16},{24,20},{28,24},{5,1},{9,5},{13... | collective-permute-start | bytes 46088 | tf_op jit(solution)/shard_map/ppermute | solution.py:16
  705.2 264.6 %all-reduce.8.cloned.1.call-start = ((), (), s32[]{:S(2)}) async-start(), calls=%async_computation.8 | async-start | bytes 8650752 | tf_op jit(solution)/shard_map/psum | solution.py:315
  705.4 19.9 %slice-start = ((s8[6291456]{0:T(1024)(128)(4,1)}), s8[4194304]{0:T(1024)(128)(4,1)S(1)}, s32[]{:S(2)}) async-start(s8[6291456]{0:T(1024)(128)(4,1)} %bitcast.395), calls=%async_computation.9 | async-start | bytes 8388608
  705.5 19.9 %slice-start.4 = ((s8[5242880]{0:T(1024)(128)(4,1)}), s8[4194304]{0:T(1024)(128)(4,1)S(1)}, s32[]{:S(2)}) async-start(s8[5242880]{0:T(1024)(128)(4,1)} %bitcast.412), calls=%async_computation.13 | async-start | bytes 8388608
  802.8 57.8 %copy-start.37 = (bf16[2,2048,192]{1,2,0:T(8,128)(2,1)S(1)}, bf16[2,2048,192]{1,2,0:T(8,128)(2,1)}, u32[]{:S(2)}) copy-start(bf16[2,2048,192]{1,2,0:T(8,128)(2,1)} %param.34) | copy-start | bytes 4718596
  802.8 57.8 %copy-start.56 = (f32[2,2048]{1,0:T(2,128)S(1)}, f32[2,2048]{1,0:T(2,128)}, u32[]{:S(2)}) copy-start(f32[2,2048]{1,0:T(2,128)} %copy-done.55) | copy-start | bytes 49156
  860.7 115.9 %copy-start.1 = (bf16[768,384]{1,0:T(8,128)(2,1)S(1)}, bf16[768,384]{1,0:T(8,128)(2,1)}, u32[]{:S(2)}) copy-start(bf16[768,384]{1,0:T(8,128)(2,1)} %param.36) | copy-start | bytes 1769476
  (102 other events, 779.3 us)
Sparse Core Ops, SparseCore 0:
  118.2 60.0 all-gather.3
  179.9 44.9 all-gather.5
  286.3 59.5 all-gather.7
  403.1 81.8 all-reduce.5
  487.6 99.1 reduce-scatter.2
  705.3 97.4 reduce-scatter.4
  808.5 161.3 all-reduce.7
where the time goes:
time: 996 us; the launch traced here: 984 us
  local copies, waits for them, and re-layouts  246 us (25%)
  other arithmetic  234 us (23%)
  matrix products  197 us (20%)
  waiting for transfers between devices  171 us (17%)
  blocking collectives  110 us (11%)
  between operations  16.2 us (2%)
    scatter-add x3, local copies, waits for them, and re-layouts, shards(): d_pad.at[:, tap_index:tap_index + tokens]  118 us
    psum x1, waiting for transfers between devices, shards(): lax.psum((input_gain_gradient, grad_z, grad_x, grad_bc, grad_dt, grad_con...  104 us
    reduce_scatter x1, waiting for transfers between devices, shards(): lax.psum_scatter(partial_in, 'head', scatter_dimension=2, tiled=True)  50.8 us
    psum x1, blocking collectives, shards(): lax.psum((input_gain_gradient, grad_z, grad_x, grad_bc, grad_dt, grad_con...  40.6 us
    all_gather x2, blocking collectives, prefix(): everything = jax.tree.map(lambda part: lax.all_gather(part, axis), x)  38.5 us
    add x3, other arithmetic, shards(): d_pad.at[:, tap_index:tap_index + tokens]  36.3 us
    unnamed x298, local copies, waits for them, and re-layouts  35.3 us
    reduce_sum x1, other arithmetic, shards(): jnp.sum(masked * conv_pad[:, tap_index:tap_index + tokens].astype(jnp.flo...  23.9 us
  transfers between devices with their start and end apart: 9, of which 3 were waited for; matrix products, arithmetic and copies ran while one was open for 53% of the time, Pallas kernels for 0%

commit v1 on v0

v1 whole, which is shorter than its diff:
```python
import functools

import jax
import jax.numpy as jnp
import numpy as np
from jax import lax
from jax.experimental import pallas as pl
from jax.experimental.pallas import tpu as pltpu
from jax.sharding import PartitionSpec as P

GROUP = 256
HALF = 128
LANES = 128
HEAD_DIM = 64
EPS = 1e-05
LOG2E = 1.4426950408889634
f32 = jnp.float32
bf16 = jnp.bfloat16
HIGHEST = lax.Precision.HIGHEST
ROWS = 32


def dot(a, b, ca=1, cb=0, precision=None):
    return lax.dot_general(
        a, b, (((ca,), (cb,)), ((), ())), precision=precision, preferred_element_type=f32
    )


def split2(x):
    hi = x.astype(bf16)
    return hi, (x - hi.astype(f32)).astype(bf16)


def expand(x, ex):
    hi = x.astype(bf16).astype(f32)
    rest = x - hi
    mid = rest.astype(bf16).astype(f32)
    low = rest - mid
    packed = hi + pltpu.roll(mid, 32, 1) + pltpu.roll(low, 64, 1)
    return dot(packed.astype(bf16), ex)


def lanes_below(x, count):
    return jnp.where(lax.broadcasted_iota(jnp.int32, x.shape, 1) < count, x, 0.0)


def sigmoid(x):
    return 1.0 / (1.0 + jnp.exp(-x))


def softplus(x):
    return jnp.maximum(x, 0.0) + jnp.log1p(jnp.exp(-jnp.abs(x)))


def fold8(x):
    total = x[0:8]
    for r in range(8, x.shape[0], 8):
        total = total + x[r : r + 8]
    return total


def expansion(width):
    heads = width // HEAD_DIM
    ex = np.zeros((LANES, width), np.float32)
    for part in range(3):
        for h in range(heads):
            ex[32 * part + h, h * HEAD_DIM : (h + 1) * HEAD_DIM] = 1.0
    red = np.zeros((width, LANES), np.float32)
    for h in range(heads):
        red[h * HEAD_DIM : (h + 1) * HEAD_DIM, h] = 1.0
    return jnp.asarray(ex, bf16), jnp.asarray(red, bf16)


def run(kernel, grid, ins, outs, scratch=(), flops=0, moved=0, prefetch=()):
    def spec(shape, block, imap):
        if block is None:
            rank = len(shape)
            return pl.BlockSpec(shape, lambda *_: (0,) * rank)
        return pl.BlockSpec(block, imap)

    return pl.pallas_call(
        kernel,
        grid_spec=pltpu.PrefetchScalarGridSpec(
            num_scalar_prefetch=len(prefetch),
            grid=grid,
            in_specs=[spec(a.shape, b, m) for a, b, m in ins],
            out_specs=[spec(s, b, m) for s, _, b, m in outs],
            scratch_shapes=list(scratch),
        ),
        out_shape=[jax.ShapeDtypeStruct(s, d) for s, d, _, _ in outs],
        compiler_params=pltpu.CompilerParams(vmem_limit_bytes=56 << 20),
        cost_estimate=pl.CostEstimate(flops=flops, bytes_accessed=moved, transcendentals=0),
    )(*prefetch, *[a for a, _, _ in ins])


def conv_rows(ext, age, taps, bias, r, cols):
    acc = jnp.broadcast_to(bias[:, cols], (ROWS, LANES))
    for k in range(4):
        back = 3 - k
        term = ext[8 + r - back : 8 + r - back + ROWS, cols] * taps[k : k + 1, cols]
        if back:
            term = jnp.where(age >= back, term, 0.0)
        acc = acc + term
    return acc


def norm_kernel(
    meta, hid, edge, gain, bc, taps, bias, age, normed, nedge, ci, co, bmat, cmat, ext
):
    def rms(x):
        x = x.astype(f32)
        r = lax.rsqrt(jnp.sum(x * x, axis=1, keepdims=True) / x.shape[1] + EPS)
        return (x * r * gain[...]).astype(bf16)

    @pl.when(pl.program_id(0) == 0)
    def _():
        rows = rms(edge[...])
        nedge[...] = rows
        ext[0:8] = dot(rows, bc[...]).astype(bf16).astype(f32)[8:16]

    @pl.when(pl.program_id(0) > 0)
    def _():
        ext[0:8] = ext[GROUP : GROUP + 8]

    for r in range(0, GROUP, ROWS):
        normed[r : r + ROWS] = rms(hid[0, r : r + ROWS])
    low = dot(normed[...], bc[...]).astype(bf16)
    ci[...] = low
    ext[8 : 8 + GROUP] = low.astype(f32)
    for r in range(0, GROUP, ROWS):
        a = age[r : r + ROWS]
        for j, out in enumerate((bmat, cmat)):
            cols = slice(j * LANES, (j + 1) * LANES)
            v = conv_rows(ext, a, taps, bias, r, cols)
            co[r : r + ROWS, cols] = v
            out[r : r + ROWS] = (v * sigmoid(v)).astype(bf16)


def front_kernel(
    normed, nedge, wa, wb, taps, bias, dtp, dtb, rate, bmat, age, tril, ex,
    ci, co, val, pre, cum, lin, kb, ck, tot, ktot,
    ext, running, kept, omx, ohi, olo,
):
    i = pl.program_id(0)
    width = val.shape[1]
    part = width // 2

    @pl.when(i == 0)
    def _():
        running[...] = jnp.zeros_like(running)
        kept[...] = jnp.ones_like(kept)
        for w, at in ((wa, 0), (wb, part)):
            ext[0:8, at : at + part] = dot(nedge[...], w[...]).astype(bf16).astype(f32)[8:16]

    @pl.when(i > 0)
    def _():
        ext[0:8] = ext[GROUP : GROUP + 8]

    for w, at in ((wa, 0), (wb, part)):
        low = dot(normed[...], w[...]).astype(bf16)
        ci[:, at : at + part] = low
        ext[8 : 8 + GROUP, at : at + part] = low.astype(f32)
    raw = dot(normed[...], dtp[...], 1, 1) + dtb[...]
    pre[...] = raw
    delta = softplus(raw)
    c = dot(tril[...], delta * rate[...], precision=HIGHEST)
    cum[...] = c
    end = c[GROUP - 1 : GROUP]
    age_end = age[GROUP - 1 : GROUP]
    left = GROUP - 1 - lax.broadcasted_iota(jnp.int32, c.shape, 0)
    omega = jnp.where(left <= age_end, jnp.exp(end - c), 0.0) * delta
    omx[...] = expand(lanes_below(omega, width // HEAD_DIM), ex[...])
    keep = jnp.where(age_end >= GROUP, jnp.exp(end), 0.0)
    keep = lanes_below(jnp.broadcast_to(keep, (8, LANES)), width // HEAD_DIM)
    keepx = expand(keep, ex[...])
    for r in range(0, GROUP, ROWS):
        a = age[r : r + ROWS]
        rows = slice(r, r + ROWS)
        for j in range(width // LANES):
            cols = slice(j * LANES, (j + 1) * LANES)
            v = conv_rows(ext, a, taps, bias, r, cols)
            co[rows, cols] = v
            act = (v * sigmoid(v)).astype(bf16)
            val[rows, cols] = act
            ohi[rows, cols], olo[rows, cols] = split2(omx[rows, cols] * act.astype(f32))
    own = dot(bmat[...], ohi[...], 0, 0) + dot(bmat[...], olo[...], 0, 0)
    lin[0] = running[...]
    kb[0] = kept[...]
    ck[0] = keepx
    running[...] = keepx[0:1] * running[...] + own
    kept[...] = keepx * kept[...]
    tot[...] = running[...]
    ktot[...] = kept[...]


def pair_masks(x, lane_axis_shape):
    lane = lax.broadcasted_iota(jnp.int32, lane_axis_shape, 1)
    zero = jnp.zeros_like(x)
    return jnp.where(lane < HEAD_DIM, x, zero), jnp.where(lane >= HEAD_DIM, x, zero)


def intra_kernel(val, bmat, cmat, age, pre, cum, dskip, part):
    t = lax.broadcasted_iota(jnp.int32, (HALF, HALF), 0)
    s = lax.broadcasted_iota(jnp.int32, (HALF, HALF), 1)
    scores = dot(cmat[...], bmat[...], 1, 1)
    a0, a1 = age[0:HALF], age[HALF:]
    gap = t - s
    s00 = jnp.where((gap >= 0) & (gap <= a0), scores[:HALF, :HALF], 0.0)
    s11 = jnp.where((gap >= 0) & (gap <= a1), scores[HALF:, HALF:], 0.0)
    s10 = jnp.where(gap + HALF <= a1, scores[HALF:, :HALF], 0.0)
    c2 = cum[...] * LOG2E
    rows = (c2 - jnp.log2(softplus(pre[...]))).T
    for j in range(val.shape[1] // LANES):
        cols = slice(j * LANES, (j + 1) * LANES)
        v = val[:, cols]
        vm = pair_masks(v, v.shape)
        tops, bottoms = [], []
        for which in range(2):
            h = 2 * j + which
            col0 = jnp.broadcast_to(c2[:HALF, h : h + 1], (HALF, HALF))
            col1 = jnp.broadcast_to(c2[HALF:, h : h + 1], (HALF, HALF))
            r0 = rows[h : h + 1, :HALF]
            r1 = rows[h : h + 1, HALF:]
            tops.append((s00 * jnp.exp2(jnp.minimum(col0 - r0, 60.0))).astype(bf16))
            bottoms.append((s10 * jnp.exp2(col1 - r0)).astype(bf16))
            bottoms.append((s11 * jnp.exp2(jnp.minimum(col1 - r1, 60.0))).astype(bf16))
        top = dot(jnp.concatenate(tops, axis=1), jnp.concatenate([vm[0][:HALF], vm[1][:HALF]], axis=0))
        bottom = dot(jnp.concatenate(bottoms, axis=1), jnp.concatenate([vm[0], vm[1]], axis=0))
        skip = dskip[:, cols]
        part[:HALF, cols] = top + skip * v[:HALF].astype(f32)
        part[HALF:, cols] = bottom + skip * v[HALF:].astype(f32)


def mid_kernel(
    meta, hid, normed, z0, z1, z2, z3, o0, o1, o2, o3, cot, cmat, age, ex, red, gain,
    part_a, part_b, val_a, val_b, cum_a, cum_b, lin_a, lin_b, kb_a, kb_b, ck_a, ck_b, arr_a, arr_b,
    pieces, nout, cotx, dssd, dgate, dcin, dkk_a, dkk_b,
    lout_a, lout_b, ka_a, ka_b, tot_a, tot_b, ktot_a, ktot_b, ggain, gskip,
    gate, dno, read, kx, ssd_s, sig_s, khi, klo, rhi, rlo, run_a, run_b, kept_a, kept_b,
):
    i = pl.program_id(0)
    inner = nout.shape[1]
    width = inner // 2
    tiles = inner // LANES
    heads = width // HEAD_DIM
    quarter = inner // 4

    @pl.when(i == 0)
    def _():
        for ref in (run_a, run_b, ggain, gskip):
            ref[...] = jnp.zeros_like(ref)
        for ref in (kept_a, kept_b):
            ref[...] = jnp.ones_like(ref)

    cotan = jnp.concatenate([cot[0], cot[1], cot[2], cot[3]], axis=1)
    cotx[...] = cotan
    states = []
    for half, (lin, kb, arr, cum) in enumerate(
        ((lin_a, kb_a, arr_a, cum_a), (lin_b, kb_b, arr_b, cum_b))
    ):
        cols = slice(half * width, (half + 1) * width)
        hi, lo = split2(lin[0] + kb[0, 0:1] * arr[...])
        states.append((hi, lo))
        read[:, cols] = dot(cmat[...], hi) + dot(cmat[...], lo)
        since = lax.broadcasted_iota(jnp.int32, age.shape, 0)
        kappa = jnp.where(age[...] > since, jnp.exp(cum[...]), 0.0)
        kx[:, cols] = expand(lanes_below(kappa, heads), ex[...])
    for k, (z, o) in enumerate(((z0, o0), (z1, o1), (z2, o2), (z3, o3))):
        cols = slice(k * quarter, (k + 1) * quarter)
        gate[:, cols] = dot(normed[...], z[...])
        dno[:, cols] = dot(cotan, o[...], 1, 1)

    def rows_body(step, _):
        rows = pl.ds(pl.multiple_of(step * ROWS, ROWS), ROWS)
        squares = jnp.zeros((ROWS, LANES), f32)
        inners = jnp.zeros((ROWS, LANES), f32)
        for j in range(tiles):
            cols = slice(j * LANES, (j + 1) * LANES)
            part = part_a if j < tiles // 2 else part_b
            pcols = slice(cols.start % width, cols.start % width + LANES)
            ssd = part[rows, pcols] + kx[rows, cols] * read[rows, cols]
            g = gate[rows, cols]
            sig = sigmoid(g)
            gated = ssd * (g * sig)
            squares += gated * gated
            inners += gated * (dno[rows, cols] * gain[:, cols])
            ssd_s[rows, cols] = ssd
            sig_s[rows, cols] = sig
        rg = lax.rsqrt(jnp.sum(squares, axis=1, keepdims=True) / inner + EPS)
        stat = rg * rg * (jnp.sum(inners, axis=1, keepdims=True) / inner)
        rg = jnp.broadcast_to(rg, (ROWS, LANES))
        stat = jnp.broadcast_to(stat, (ROWS, LANES))
        for j in range(tiles):
            cols = slice(j * LANES, (j + 1) * LANES)
            val = val_a if j < tiles // 2 else val_b
            pcols = slice(cols.start % width, cols.start % width + LANES)
            ssd, sig, g, d = ssd_s[rows, cols], sig_s[rows, cols], gate[rows, cols], dno[rows, cols]
            act = g * sig
            gated = ssd * act
            yhat = gated * rg
            nout[rows, cols] = (yhat * gain[:, cols]).astype(bf16)
            ggain[:, cols] += fold8(d * yhat)
            dgated = rg * (d * gain[:, cols] - gated * stat)
            low = (dgated * act).astype(bf16)
            dssd[rows, cols] = low
            dgate[rows, cols] = (dgated * ssd * (sig * (1.0 + g * (1.0 - sig)))).astype(bf16)
            dy = low.astype(f32)
            gskip[:, cols] += fold8(dy * val[rows, pcols].astype(f32))
            kd = kx[rows, cols] * dy
            khi[rows, cols], klo[rows, cols] = split2(kd)
            rhi[rows, cols], rlo[rows, cols] = split2(kd * read[rows, cols])
        return 0

    lax.fori_loop(0, GROUP // ROWS, rows_body, 0)
    out = hid[0].astype(f32)
    for k, o in enumerate((o0, o1, o2, o3)):
        out = out + dot(nout[:, k * quarter : (k + 1) * quarter], o[...])
    out = out.astype(bf16)
    piece = out.shape[1] // 4
    for k in range(4):
        pieces[k] = out[:, k * piece : (k + 1) * piece]
    dc = None
    for half, (dkk, ck, lout, ka, tot, ktot, running, kept) in enumerate(
        (
            (dkk_a, ck_a, lout_a, ka_a, tot_a, ktot_a, run_a, kept_a),
            (dkk_b, ck_b, lout_b, ka_b, tot_b, ktot_b, run_b, kept_b),
        )
    ):
        cols = slice(half * width, (half + 1) * width)
        hi, lo = states[half]
        dkk[...] = dot(rhi[:, cols], red[...]) + dot(rlo[:, cols], red[...])
        term = dot(khi[:, cols], hi, 1, 1) + dot(khi[:, cols], lo, 1, 1) + dot(klo[:, cols], hi, 1, 1)
        dc = term if dc is None else dc + term
        own = dot(cmat[...], khi[:, cols], 0, 0) + dot(cmat[...], klo[:, cols], 0, 0)
        lout[0] = running[...]
        ka[0] = kept[...]
        running[...] = ck[0, 0:1] * running[...] + own
        kept[...] = ck[0] * kept[...]
        tot[...] = running[...]
        ktot[...] = kept[...]
    dcin[...] = dc


def pairs_kernel(val, dssd, bmat, cmat, ager, pre, cum, dvi, dbi, dci, rflow, cflow, rft):
    s = lax.broadcasted_iota(jnp.int32, (HALF, HALF), 0)
    t = lax.broadcasted_iota(jnp.int32, (HALF, HALF), 1)
    scores = dot(bmat[...], cmat[...], 1, 1)
    a0, a1 = ager[0:1, :HALF], ager[0:1, HALF:]
    gap = t - s
    m00 = (gap >= 0) & (gap <= a0)
    m11 = (gap >= 0) & (gap <= a1)
    m01 = gap + HALF <= a1
    s00 = jnp.where(m00, scores[:HALF, :HALF], 0.0)
    s11 = jnp.where(m11, scores[HALF:, HALF:], 0.0)
    s01 = jnp.where(m01, scores[:HALF, HALF:], 0.0)
    c2 = cum[...] * LOG2E
    cr = c2 - jnp.log2(softplus(pre[...]))
    c2t = c2.T
    lane = lax.broadcasted_iota(jnp.int32, (HALF, LANES), 1)
    zero = jnp.zeros((HALF, HALF), f32)
    d00, d01, d11 = zero, zero, zero
    cf0, cf1 = zero, zero
    rft[...] = jnp.zeros_like(rft)
    for j in range(val.shape[1] // LANES):
        cols = slice(j * LANES, (j + 1) * LANES)
        v = val[:, cols]
        dy = dssd[:, cols]
        vm = pair_masks(v, v.shape)
        dm = pair_masks(dy, dy.shape)
        tops, bottoms = [], []
        for which in range(2):
            h = 2 * j + which
            col0 = jnp.broadcast_to(cr[:HALF, h : h + 1], (HALF, HALF))
            col1 = jnp.broadcast_to(cr[HALF:, h : h + 1], (HALF, HALF))
            r0 = c2t[h : h + 1, :HALF]
            r1 = c2t[h : h + 1, HALF:]
            e00 = jnp.exp2(jnp.minimum(r0 - col0, 60.0))
            e01 = jnp.exp2(r1 - col0)
            e11 = jnp.exp2(jnp.minimum(r1 - col1, 60.0))
            tops.append((s00 * e00).astype(bf16))
            tops.append((s01 * e01).astype(bf16))
            bottoms.append((s11 * e11).astype(bf16))
            w0 = dot(vm[which][:HALF], dy, 1, 1)
            w1 = dot(vm[which][HALF:], dy[HALF:], 1, 1)
            de00 = w0[:, :HALF] * e00
            de01 = w0[:, HALF:] * e01
            de11 = w1 * e11
            d00 += de00
            d01 += de01
            d11 += de11
            f00 = de00 * s00
            f01 = de01 * s01
            f11 = de11 * s11
            rft[h : h + 1, :HALF] = jnp.sum(f00, axis=0, keepdims=True)
            rft[h : h + 1, HALF:] = jnp.sum(f01 + f11, axis=0, keepdims=True)
            cf0 = jnp.where(lane == h, jnp.sum(f00 + f01, axis=1, keepdims=True), cf0)
            cf1 = jnp.where(lane == h, jnp.sum(f11, axis=1, keepdims=True), cf1)
        dvi[:HALF, cols] = dot(jnp.concatenate(tops, axis=1), jnp.concatenate([dm[0], dm[1]], axis=0))
        dvi[HALF:, cols] = dot(
            jnp.concatenate(bottoms, axis=1), jnp.concatenate([dm[0][HALF:], dm[1][HALF:]], axis=0)
        )
    cflow[:HALF] = cf0
    cflow[HALF:] = cf1
    rflow[...] = rft[...].T
    d00 = split2(jnp.where(m00, d00, 0.0))
    d01 = split2(jnp.where(m01, d01, 0.0))
    d11 = split2(jnp.where(m11, d11, 0.0))
    b0, b1, c0, c1 = bmat[:HALF], bmat[HALF:], cmat[:HALF], cmat[HALF:]
    dbi[:HALF] = dot(d00[0], c0) + dot(d00[1], c0) + dot(d01[0], c1) + dot(d01[1], c1)
    dbi[HALF:] = dot(d11[0], c1) + dot(d11[1], c1)
    dci[:HALF] = dot(d00[0], b0, 0, 0) + dot(d00[1], b0, 0, 0)
    dci[HALF:] = (
        dot(d01[0], b0, 0, 0) + dot(d01[1], b0, 0, 0) + dot(d11[0], b1, 0, 0) + dot(d11[1], b1, 0, 0)
    )


def slope(x):
    sig = sigmoid(x)
    return sig * (1.0 + x * (1.0 - sig))


def conv_back(i, dco, agex, age, ci, taps, dci, tail, head, gw):
    width = ci.shape[1]
    for r in range(0, GROUP, ROWS):
        ages = [agex[r + m : r + m + ROWS] for m in range(4)]
        for j in range(width // LANES):
            cols = slice(j * LANES, (j + 1) * LANES)
            c = ci[r : r + ROWS, cols].astype(f32)
            acc = None
            for m in range(4):
                x = dco[r + m : r + m + ROWS, cols]
                if m:
                    x = jnp.where(ages[m] >= m, x, 0.0)
                term = x * taps[3 - m : 4 - m, cols]
                acc = term if acc is None else acc + term
                gw[8 * (3 - m) : 8 * (3 - m) + 8, cols] += fold8(x * c)
            dci[r : r + ROWS, cols] = acc.astype(bf16)
            if r == GROUP - ROWS:

                @pl.when(i == 0)
                def _():
                    tail[:, cols] = acc[ROWS - 8 :]

    head[...] = dco[0:8]


def start_next(i, dco, agex, gw, gb):
    @pl.when(i == 0)
    def _():
        dco[GROUP : GROUP + 8] = jnp.zeros((8, dco.shape[1]), f32)
        agex[GROUP : GROUP + 8] = jnp.zeros((8, LANES), jnp.int32)
        gw[...] = jnp.zeros_like(gw)
        gb[...] = jnp.zeros_like(gb)

    @pl.when(i > 0)
    def _():
        dco[GROUP : GROUP + 8] = dco[0:8]
        agex[GROUP : GROUP + 8] = agex[0:8]


def back_kernel(
    val, dssd, dvi, bmat, co, ci, age, pre, cum, lout, ka, leav, lin, kb, arr, ck, rflow, cflow, dkk,
    dskip, taps, rate, tril, ex, red,
    dci, tail, head, dbin, draw, gw, gb, galog, gdtb,
    dco, agex, back, omx, ohi, olo, vhi, vlo,
):
    i = pl.program_id(0)
    width = val.shape[1]
    heads = width // HEAD_DIM
    start_next(i, dco, agex, gw, gb)

    @pl.when(i == 0)
    def _():
        galog[...] = jnp.zeros_like(galog)
        gdtb[...] = jnp.zeros_like(gdtb)

    agex[0:GROUP] = age[...]
    ds = lout[0] + ka[0, 0:1] * leav[...]
    dhi, dlo = split2(ds)
    back[...] = dot(bmat[...], dhi) + dot(bmat[...], dlo)
    p = pre[...]
    delta = softplus(p)
    c = cum[...]
    end = c[GROUP - 1 : GROUP]
    age_end = age[GROUP - 1 : GROUP]
    row = lax.broadcasted_iota(jnp.int32, c.shape, 0)
    tail_keep = jnp.where(GROUP - 1 - row <= age_end, jnp.exp(end - c), 0.0)
    omega = tail_keep * delta
    omx[...] = expand(lanes_below(omega, heads), ex[...])
    for r in range(0, GROUP, ROWS):
        rows = slice(r, r + ROWS)
        for j in range(width // LANES):
            cols = slice(j * LANES, (j + 1) * LANES)
            v = val[rows, cols].astype(f32)
            b = back[rows, cols]
            o = omx[rows, cols]
            dval = dskip[:, cols] * dssd[rows, cols].astype(f32) + dvi[rows, cols] + o * b
            ohi[rows, cols], olo[rows, cols] = split2(o * v)
            vhi[rows, cols], vlo[rows, cols] = split2(v * b)
            d = dval * slope(co[rows, cols])
            dco[rows, cols] = d
            gb[:, cols] += fold8(d)
    dbin[...] = dot(ohi[...], dhi, 1, 1) + dot(ohi[...], dlo, 1, 1) + dot(olo[...], dhi, 1, 1)
    domega = dot(vhi[...], red[...]) + dot(vlo[...], red[...])
    flow = domega * omega
    sin = lin[0] + kb[0, 0:1] * arr[...]
    carry = jnp.broadcast_to(jnp.sum(ds * sin, axis=0, keepdims=True), (8, width))
    carry = dot(carry, red[...].astype(f32), precision=HIGHEST)[0:1]
    keep = jnp.where(age_end >= GROUP, jnp.exp(end), 0.0)
    dcum = rflow[...] - cflow[...] + dkk[...] - flow
    ending = jnp.sum(flow, axis=0, keepdims=True) + carry * keep
    dcum = dcum + jnp.where(row == GROUP - 1, ending, 0.0)
    dlog = dot(tril[...], dcum, 0, 0, precision=HIGHEST)
    sig = sigmoid(p)
    ratio = jnp.where(delta > 1e-30, sig / delta, 1.0)
    drf = cflow[...] * ratio + (domega * tail_keep + dlog * rate[...]) * sig
    drf = lanes_below(drf, heads)
    draw[...] = drf.astype(bf16)
    gdtb[...] += fold8(drf)
    galog[...] += fold8(dlog * delta)
    conv_back(i, dco, agex, age, ci, taps, dci, tail, head, gw)


def maps_kernel(
    dbi_a, dbi_b, dbin_a, dbin_b, dci_a, dci_b, dcin, co, ci, age, taps, dci, tail, head, gw, gb, dco, agex
):
    i = pl.program_id(0)
    start_next(i, dco, agex, gw, gb)
    agex[0:GROUP] = age[...]
    for r in range(0, GROUP, ROWS):
        rows = slice(r, r + ROWS)
        db = dbi_a[rows] + dbi_b[rows] + dbin_a[rows] + dbin_b[rows]
        dc = dci_a[rows] + dci_b[rows] + dcin[rows]
        for j, d in enumerate((db, dc)):
            cols = slice(j * LANES, (j + 1) * LANES)
            d = d * slope(co[rows, cols])
            dco[rows, cols] = d
            gb[:, cols] += fold8(d)
    conv_back(i, dco, agex, age, ci, taps, dci, tail, head, gw)


def final_kernel(
    meta, hid, cotx, gain, dgate, z0, z1, z2, z3, dx_a, dx_b, x0, x1, x2, x3, dbc, bc, dr_a, dr_b, dt_a, dt_b,
    pieces, ggain, acc_s,
):
    @pl.when(pl.program_id(0) == 0)
    def _():
        ggain[...] = jnp.zeros_like(ggain)

    quarter = z0.shape[1]
    acc = dot(dbc[...], bc[...], 1, 1) + dot(dr_a[...], dt_a[...]) + dot(dr_b[...], dt_b[...])
    for k, (z, x) in enumerate(((z0, x0), (z1, x1), (z2, x2), (z3, x3))):
        acc = acc + dot(dgate[:, k * quarter : (k + 1) * quarter], z[...], 1, 1)
        dx = dx_a if k < 2 else dx_b
        at = (k % 2) * quarter
        acc = acc + dot(dx[:, at : at + quarter], x[...], 1, 1)
    acc_s[...] = acc
    piece = acc.shape[1] // 4
    for r in range(0, GROUP, ROWS):
        rows = slice(r, r + ROWS)
        x = hid[0, rows].astype(f32)
        rinv = lax.rsqrt(jnp.sum(x * x, axis=1, keepdims=True) / x.shape[1] + EPS)
        xhat = x * rinv
        d = acc_s[rows]
        ggain[...] += fold8(d * xhat)
        dx = d * gain[...]
        mean = jnp.sum(dx * xhat, axis=1, keepdims=True) / x.shape[1]
        out = (cotx[rows].astype(f32) + rinv * (dx - xhat * mean)).astype(bf16)
        for k in range(4):
            pieces[k, rows] = out[:, k * piece : (k + 1) * piece]


def scan_kernel(reverse, n, x, keep, out):
    state = jnp.zeros(x.shape[1:], f32)
    for step in range(n):
        at = n - 1 - step if reverse else step
        out[at] = state
        if step < n - 1:
            state = keep[at] * state + x[at]


def shards(
    hidden_in,
    output_cotangent,
    input_norm_scale_gain,
    z_proj,
    x_proj,
    bc_proj,
    dt_proj,
    conv_x_weight,
    conv_x_bias,
    conv_bc_weight,
    conv_bc_bias,
    dt_bias,
    a_log,
    d_skip,
    out_norm_gain,
    out_proj,
    doc_starts,
):
    batch, tokens, features = hidden_in.shape
    quarter = z_proj.shape[1]
    width = 2 * quarter
    inner = 4 * quarter
    heads = dt_proj.shape[1]
    seqs = lax.axis_size("seq")
    head_devices = lax.axis_size("head")
    parts = head_devices // batch
    chunk = tokens // parts
    count = chunk // GROUP
    si, hi_ = lax.axis_index("seq"), lax.axis_index("head")
    seq_of, half = hi_ // parts, hi_ % parts
    meta = jnp.stack([seq_of, half * count]).astype(jnp.int32)
    core = [(h, h ^ 1) for h in range(head_devices)]
    across = [(h, h ^ 2) for h in range(head_devices)]

    def swap(x):
        return lax.ppermute(x, "head", core)

    def cross(x):
        return lax.ppermute(x, "head", across)

    def spread(x):
        x2 = cross(x)
        return [x, swap(x), x2, swap(x2)]

    small = jnp.concatenate(
        [
            conv_x_weight.T,
            conv_x_bias[None],
            out_norm_gain[None],
            jnp.pad(jnp.concatenate([dt_bias, a_log, d_skip])[None], ((0, 1), (0, quarter - 3 * heads))),
            jnp.pad(dt_proj.T.astype(f32), ((0, 8 - heads), (0, 0))).reshape(8 * features // quarter, quarter),
        ],
        axis=0,
    )
    edge = jnp.where(
        half == 0,
        lax.ppermute(
            lax.dynamic_slice(hidden_in, (seq_of, tokens - 16, 0), (1, 16, features))[0],
            "seq",
            [(s, s + 1) for s in range(seqs - 1)],
        ),
        lax.dynamic_slice(hidden_in, (seq_of, chunk - 16, 0), (1, 16, features))[0],
    )
    smalls = spread(small)
    xs = spread(x_proj)
    zs = spread(z_proj)
    os_ = spread(out_proj)
    cots = lax.all_to_all(
        output_cotangent.reshape(head_devices, chunk, features // head_devices), "head", 0, 0
    )

    first_pos = si * tokens + half * chunk
    places = first_pos + jnp.arange(chunk, dtype=jnp.int32)
    starts = lax.dynamic_slice(doc_starts, (seq_of, 0), (1, doc_starts.shape[1]))[0]
    first = jnp.max(jnp.where(starts[None, :] <= places[:, None], starts[None, :], 0), axis=1)
    age1 = places - first
    age = jnp.broadcast_to(age1[:, None], (chunk, LANES))
    ager = jnp.broadcast_to(age1[None, :], (8, chunk))

    ex, red = expansion(width)
    tril = jnp.asarray(np.tril(np.ones((GROUP, GROUP), np.float32)))
    hid_map = lambda i, m: (m[0], m[1] + i, 0)
    here = lambda i, *_: (i, 0)
    gain_in = input_norm_scale_gain[None]

    taps_bc = conv_bc_weight.T
    normed, nedge, ci_bc, co_bc, bmat, cmat = run(
        norm_kernel,
        (count,),
        [
            (hidden_in, (1, GROUP, features), hid_map),
            (edge, None, None),
            (gain_in, None, None),
            (bc_proj, None, None),
            (taps_bc, None, None),
            (conv_bc_bias[None], None, None),
            (age, (GROUP, LANES), here),
        ],
        [
            ((chunk, features), bf16, (GROUP, features), here),
            ((16, features), bf16, None, None),
            ((chunk, 2 * LANES), bf16, (GROUP, 2 * LANES), here),
            ((chunk, 2 * LANES), f32, (GROUP, 2 * LANES), here),
            ((chunk, LANES), bf16, (GROUP, LANES), here),
            ((chunk, LANES), bf16, (GROUP, LANES), here),
        ],
        [pltpu.VMEM((GROUP + 8, 2 * LANES), f32)],
        flops=2 * chunk * features * 256,
        moved=6_000_000,
        prefetch=(meta,),
    )

    def join(k, rows):
        return jnp.concatenate([smalls[k][rows], smalls[k + 1][rows]], axis=1)

    def lane_pack(k, at):
        row = jnp.concatenate(
            [smalls[k][6, at * heads : (at + 1) * heads], smalls[k + 1][6, at * heads : (at + 1) * heads]]
        )
        return jnp.pad(row, (0, LANES - 2 * heads))[None]

    halves = []
    for k in (0, 2):
        taps = join(k, slice(0, 4))
        bias = join(k, slice(4, 5))
        dtp = jnp.concatenate(
            [smalls[k + n][8:].reshape(8, features)[:heads] for n in range(2)], axis=0
        ).astype(bf16)
        dtp = jnp.pad(dtp, ((0, LANES - 2 * heads), (0, 0)))
        rate = -jnp.exp(lane_pack(k, 1))
        dskip = jnp.repeat(lane_pack(k, 2)[0, : 2 * heads], HEAD_DIM)[None]
        outs = run(
            front_kernel,
            (count,),
            [
                (normed, (GROUP, features), here),
                (nedge, None, None),
                (xs[k], None, None),
                (xs[k + 1], None, None),
                (taps, None, None),
                (bias, None, None),
                (dtp, None, None),
                (lane_pack(k, 0), None, None),
                (rate, None, None),
                (bmat, (GROUP, LANES), here),
                (age, (GROUP, LANES), here),
                (tril, None, None),
                (ex, None, None),
            ],
            [
                ((chunk, width), bf16, (GROUP, width), here),
                ((chunk, width), f32, (GROUP, width), here),
                ((chunk, width), bf16, (GROUP, width), here),
                ((chunk, LANES), f32, (GROUP, LANES), here),
                ((chunk, LANES), f32, (GROUP, LANES), here),
                ((count, LANES, width), f32, (1, LANES, width), lambda i: (i, 0, 0)),
                ((count, 8, width), f32, (1, 8, width), lambda i: (i, 0, 0)),
                ((count, 8, width), f32, (1, 8, width), lambda i: (i, 0, 0)),
                ((LANES, width), f32, None, None),
                ((8, width), f32, None, None),
            ],
            [
                pltpu.VMEM((GROUP + 8, width), f32),
                pltpu.VMEM((LANES, width), f32),
                pltpu.VMEM((8, width), f32),
                pltpu.VMEM((GROUP, width), f32),
                pltpu.VMEM((GROUP, width), bf16),
                pltpu.VMEM((GROUP, width), bf16),
            ],
            flops=2 * chunk * features * 1024 * 4,
            moved=16_000_000,
        )
        names = ("ci", "co", "val", "pre", "cum", "lin", "kb", "ck", "tot", "ktot")
        d = dict(zip(names, outs))
        d.update(taps=taps, bias=bias, dtp=dtp, rate=rate, dskip=dskip)
        halves.append(d)

    for d in halves:
        d["part"] = run(
            intra_kernel,
            (count,),
            [
                (d["val"], (GROUP, width), here),
                (bmat, (GROUP, LANES), here),
                (cmat, (GROUP, LANES), here),
                (age, (GROUP, LANES), here),
                (d["pre"], (GROUP, LANES), here),
                (d["cum"], (GROUP, LANES), here),
                (d["dskip"], None, None),
            ],
            [((chunk, width), f32, (GROUP, width), here)],
            flops=10_000_000_000,
            moved=8_000_000,
        )[0]

    def exchange(tots, ktots, reverse):
        a, b = tots
        ka, kb = ktots
        mine = jnp.concatenate(
            [
                jnp.concatenate([a[:, :quarter], b[:, :quarter]], axis=1),
                jnp.concatenate([ka[:, :quarter], kb[:, :quarter]], axis=1),
            ],
            axis=0,
        )
        other = jnp.concatenate(
            [
                jnp.concatenate([a[:, quarter:], b[:, quarter:]], axis=1),
                jnp.concatenate([ka[:, quarter:], kb[:, quarter:]], axis=1),
            ],
            axis=0,
        )
        got = swap(other)
        leads = (half == 0) if not reverse else (half == 1)
        lead = jnp.where(leads, mine, got)
        follow = jnp.where(leads, got, mine)
        lead_s, lead_k = lead[:LANES], lead[LANES : LANES + 1]
        follow_s, follow_k = follow[:LANES], follow[LANES : LANES + 1]
        chip_s = follow_k * lead_s + follow_s
        chip_k = lead_k * follow_k
        per = LANES // seqs
        keeps = lax.all_gather(chip_k, "seq", axis=0)
        spread_s = lax.all_to_all(chip_s.reshape(seqs, per, width), "seq", 0, 0)
        scanned = pl.pallas_call(
            functools.partial(scan_kernel, reverse, seqs),
            out_shape=jax.ShapeDtypeStruct((seqs, per, width), f32),
        )(spread_s, keeps)
        arriving = lax.all_to_all(scanned, "seq", 0, 0).reshape(LANES, width)
        second = lead_k * arriving + lead_s
        own = jnp.where(leads, arriving, second)
        theirs = swap(jnp.where(leads, second, arriving))
        return (
            jnp.concatenate([own[:, :quarter], theirs[:, :quarter]], axis=1),
            jnp.concatenate([own[:, quarter:], theirs[:, quarter:]], axis=1),
        )

    ha, hb = halves
    arr = exchange((ha["tot"], hb["tot"]), (ha["ktot"], hb["ktot"]), False)

    gain_out = jnp.concatenate([s[5:6] for s in smalls], axis=1)
    rev = lambda i, *_: (count - 1 - i, 0)
    rev3 = lambda i, *_: (count - 1 - i, 0, 0)
    rev_hid = lambda i, m: (m[0], m[1] + count - 1 - i, 0)
    piece = features // 4
    wide = (GROUP, inner)
    half_in = (GROUP, width)
    state_block = (1, LANES, width)
    keep_block = (1, 8, width)
    outs = run(
        mid_kernel,
        (count,),
        [
            (hidden_in, (1, GROUP, features), rev_hid),
            (normed, (GROUP, features), rev),
            *[(z, None, None) for z in zs],
            *[(o, None, None) for o in os_],
            (cots, (4, GROUP, piece), lambda i, *_: (0, count - 1 - i, 0)),
            (cmat, (GROUP, LANES), rev),
            (age, (GROUP, LANES), rev),
            (ex, None, None),
            (red, None, None),
            (gain_out, None, None),
            *[(d["part"], half_in, rev) for d in halves],
            *[(d["val"], half_in, rev) for d in halves],
            *[(d["cum"], (GROUP, LANES), rev) for d in halves],
            *[(d["lin"], state_block, rev3) for d in halves],
            *[(d["kb"], keep_block, rev3) for d in halves],
            *[(d["ck"], keep_block, rev3) for d in halves],
            *[(a, None, None) for a in arr],
        ],
        [
            ((4, chunk, piece), bf16, (4, GROUP, piece), lambda i, *_: (0, count - 1 - i, 0)),
            ((chunk, inner), bf16, wide, rev),
            ((chunk, features), bf16, (GROUP, features), rev),
            ((chunk, inner), bf16, wide, rev),
            ((chunk, inner), bf16, wide, rev),
            ((chunk, LANES), f32, (GROUP, LANES), rev),
            ((chunk, LANES), f32, (GROUP, LANES), rev),
            ((chunk, LANES), f32, (GROUP, LANES), rev),
            ((count, LANES, width), f32, state_block, rev3),
            ((count, LANES, width), f32, state_block, rev3),
            ((count, 8, width), f32, keep_block, rev3),
            ((count, 8, width), f32, keep_block, rev3),
            ((LANES, width), f32, None, None),
            ((LANES, width), f32, None, None),
            ((8, width), f32, None, None),
            ((8, width), f32, None, None),
            ((8, inner), f32, None, None),
            ((8, inner), f32, None, None),
        ],
        [pltpu.VMEM(wide, f32)] * 6
        + [pltpu.VMEM(wide, bf16)] * 4
        + [pltpu.VMEM((LANES, width), f32)] * 2
        + [pltpu.VMEM((8, width), f32)] * 2,
        flops=30_000_000_000,
        moved=50_000_000,
        prefetch=(meta,),
    )
    pieces, nout, cotx, dssd, dgate, dcin, ha["dkk"], hb["dkk"], ha["lout"], hb["lout"] = outs[:10]
    ha["ka"], hb["ka"], dtot_a, dtot_b, dk_a, dk_b, ggain_out, gskip = outs[10:]
    layer_out = lax.all_to_all(pieces, "head", 0, 0).reshape(batch, tokens, piece)

    for n, d in enumerate(halves):
        d["dvi"], d["dbi"], d["dci_c"], d["rflow"], d["cflow"] = run(
            pairs_kernel,
            (count,),
            [
                (d["val"], half_in, here),
                (dssd, half_in, lambda i, n=n: (i, n)),
                (bmat, (GROUP, LANES), here),
                (cmat, (GROUP, LANES), here),
                (ager, (8, GROUP), lambda i: (0, i)),
                (d["pre"], (GROUP, LANES), here),
                (d["cum"], (GROUP, LANES), here),
            ],
            [
                ((chunk, width), f32, half_in, here),
                ((chunk, LANES), f32, (GROUP, LANES), here),
                ((chunk, LANES), f32, (GROUP, LANES), here),
                ((chunk, LANES), f32, (GROUP, LANES), here),
                ((chunk, LANES), f32, (GROUP, LANES), here),
            ],
            [pltpu.VMEM((LANES, GROUP), f32)],
            flops=15_000_000_000,
            moved=10_000_000,
        )

    leav = exchange((dtot_a, dtot_b), (dk_a, dk_b), True)

    for n, d in enumerate(halves):
        outs = run(
            back_kernel,
            (count,),
            [
                (d["val"], half_in, rev),
                (dssd, half_in, lambda i, n=n: (count - 1 - i, n)),
                (d["dvi"], half_in, rev),
                (bmat, (GROUP, LANES), rev),
                (d["co"], half_in, rev),
                (d["ci"], half_in, rev),
                (age, (GROUP, LANES), rev),
                (d["pre"], (GROUP, LANES), rev),
                (d["cum"], (GROUP, LANES), rev),
                (d["lout"], state_block, rev3),
                (d["ka"], keep_block, rev3),
                (leav[n], None, None),
                (d["lin"], state_block, rev3),
                (d["kb"], keep_block, rev3),
                (arr[n], None, None),
                (d["ck"], keep_block, rev3),
                (d["rflow"], (GROUP, LANES), rev),
                (d["cflow"], (GROUP, LANES), rev),
                (d["dkk"], (GROUP, LANES), rev),
                (d["dskip"], None, None),
                (d["taps"], None, None),
                (d["rate"], None, None),
                (tril, None, None),
                (ex, None, None),
                (red, None, None),
            ],
            [
                ((chunk, width), bf16, half_in, rev),
                ((8, width), f32, None, None),
                ((8, width), f32, None, None),
                ((chunk, LANES), f32, (GROUP, LANES), rev),
                ((chunk, LANES), bf16, (GROUP, LANES), rev),
                ((32, width), f32, None, None),
                ((8, width), f32, None, None),
                ((8, LANES), f32, None, None),
                ((8, LANES), f32, None, None),
            ],
            [
                pltpu.VMEM((GROUP + 8, width), f32),
                pltpu.VMEM((GROUP + 8, LANES), jnp.int32),
                pltpu.VMEM(half_in, f32),
                pltpu.VMEM(half_in, f32),
            ]
            + [pltpu.VMEM(half_in, bf16)] * 4,
            flops=15_000_000_000,
            moved=20_000_000,
        )
        names = ("dx", "tail", "head", "dbin", "draw", "gw", "gb", "galog", "gdtb")
        d.update(zip(names, outs))

    dbc, tail_bc, head_bc, gw_bc, gb_bc = run(
        maps_kernel,
        (count,),
        [
            *[(d["dbi"], (GROUP, LANES), rev) for d in halves],
            *[(d["dbin"], (GROUP, LANES), rev) for d in halves],
            *[(d["dci_c"], (GROUP, LANES), rev) for d in halves],
            (dcin, (GROUP, LANES), rev),
            (co_bc, (GROUP, 2 * LANES), rev),
            (ci_bc, (GROUP, 2 * LANES), rev),
            (age, (GROUP, LANES), rev),
            (taps_bc, None, None),
        ],
        [
            ((chunk, 2 * LANES), bf16, (GROUP, 2 * LANES), rev),
            ((8, 2 * LANES), f32, None, None),
            ((8, 2 * LANES), f32, None, None),
            ((32, 2 * LANES), f32, None, None),
            ((8, 2 * LANES), f32, None, None),
        ],
        [pltpu.VMEM((GROUP + 8, 2 * LANES), f32), pltpu.VMEM((GROUP + 8, LANES), jnp.int32)],
        flops=2_000_000_000,
        moved=8_000_000,
    )

    heads_out = jnp.concatenate([ha["head"], hb["head"], head_bc], axis=1)
    heads_out = jnp.concatenate(
        [heads_out[:, 0:quarter], heads_out[:, quarter:width], heads_out[:, width:]], axis=1
    )
    pairs = []
    for s in range(seqs):
        for b in range(batch):
            for p in range(parts):
                if p > 0:
                    pairs.append((s * head_devices + b * parts + p, s * head_devices + b * parts + p - 1))
                elif s > 0:
                    pairs.append((s * head_devices + b * parts, (s - 1) * head_devices + b * parts + parts - 1))
    flipped = jnp.concatenate(
        [
            heads_out[:, quarter : 2 * quarter],
            heads_out[:, 0:quarter],
            heads_out[:, 3 * quarter : 4 * quarter],
            heads_out[:, 2 * quarter : 3 * quarter],
            heads_out[:, 4 * quarter :],
        ],
        axis=1,
    )
    got = lax.ppermute(flipped, ("seq", "head"), pairs)
    next_places = first_pos + chunk + jnp.arange(8, dtype=jnp.int32)
    next_first = jnp.max(jnp.where(starts[None, :] <= next_places[:, None], starts[None, :], 0), axis=1)
    next_age = next_places - next_first
    taps_all = jnp.concatenate([ha["taps"], hb["taps"], taps_bc], axis=1)
    tail_all = jnp.concatenate([ha["tail"], hb["tail"], tail_bc], axis=1)
    ci_all = jnp.concatenate([ha["ci"][-8:], hb["ci"][-8:], ci_bc[-8:]], axis=1).astype(f32)
    gw_fix = [jnp.zeros((tail_all.shape[1],), f32)] * 4
    for m in range(1, 4):
        masked = jnp.where((next_age >= m)[:m, None], got[:m], 0.0)
        rows = jnp.concatenate([jnp.zeros((8 - m, got.shape[1]), f32), masked], axis=0)
        tail_all = tail_all + rows * taps_all[3 - m]
        gw_fix[3 - m] = jnp.sum(rows * ci_all, axis=0)
    tail_low = tail_all.astype(bf16)
    gw_fix = jnp.stack(gw_fix)
    dxs = [
        lax.dynamic_update_slice(x, tail_low[:, at : at + x.shape[1]], (chunk - 8, 0))
        for x, at in ((ha["dx"], 0), (hb["dx"], width), (dbc, inner))
    ]

    dt_rows = [d["dtp"] for d in halves]
    in_pieces, ggain_in = run(
        final_kernel,
        (count,),
        [
            (hidden_in, (1, GROUP, features), hid_map),
            (cotx, (GROUP, features), here),
            (gain_in, None, None),
            (dgate, wide, here),
            *[(z, None, None) for z in zs],
            (dxs[0], half_in, here),
            (dxs[1], half_in, here),
            *[(x, None, None) for x in xs],
            (dxs[2], (GROUP, 2 * LANES), here),
            (bc_proj, None, None),
            (ha["draw"], (GROUP, LANES), here),
            (hb["draw"], (GROUP, LANES), here),
            (dt_rows[0], None, None),
            (dt_rows[1], None, None),
        ],
        [
            ((4, chunk, piece), bf16, (4, GROUP, piece), lambda i, *_: (0, i, 0)),
            ((8, features), f32, None, None),
        ],
        [pltpu.VMEM((GROUP, features), f32)],
        flops=12_000_000_000,
        moved=20_000_000,
        prefetch=(meta,),
    )
    input_grad = lax.all_to_all(in_pieces, "head", 0, 0).reshape(batch, tokens, piece)

    def token_dot(a, b):
        return lax.dot_general(a, b, (((0,), (0,)), ((), ())), preferred_element_type=f32)

    def reduce_slots(slots):
        one = slots[0] + swap(slots[1].astype(bf16)).astype(f32)
        two = slots[2] + swap(slots[3].astype(bf16)).astype(f32)
        return one + cross(two.astype(bf16)).astype(f32)

    def reduce_exact(slots):
        one = slots[0] + swap(slots[1])
        two = slots[2] + swap(slots[3])
        return one + cross(two)

    g_out = [token_dot(nout[:, k * quarter : (k + 1) * quarter], cotx) for k in range(4)]
    g_z = [token_dot(normed, dgate[:, k * quarter : (k + 1) * quarter]) for k in range(4)]
    g_x = [
        token_dot(normed, dxs[k // 2][:, (k % 2) * quarter : (k % 2 + 1) * quarter]) for k in range(4)
    ]
    g_bc = token_dot(normed, dxs[2])
    g_dt = [token_dot(d["draw"], normed) for d in halves]

    def slot_small(k):
        d = halves[k // 2]
        at = (k % 2) * quarter
        lane = (k % 2) * heads
        base = k // 2 * width
        gw = jnp.sum(d["gw"].reshape(4, 8, width), axis=1) + gw_fix[:, base : base + width]
        row = jnp.concatenate(
            [
                jnp.sum(d["gdtb"], axis=0)[lane : lane + heads],
                (jnp.sum(d["galog"], axis=0) * d["rate"][0])[lane : lane + heads],
                jnp.sum(
                    jnp.sum(gskip, axis=0)[k * quarter : (k + 1) * quarter].reshape(heads, HEAD_DIM), axis=1
                ),
            ]
        )
        return jnp.concatenate(
            [
                gw[:, at : at + quarter],
                jnp.sum(d["gb"], axis=0)[None, at : at + quarter],
                jnp.sum(ggain_out, axis=0)[None, k * quarter : (k + 1) * quarter],
                jnp.pad(row[None], ((0, 1), (0, quarter - 3 * heads))),
                jnp.pad(g_dt[k // 2][lane : lane + heads], ((0, 8 - heads), (0, 0))).reshape(
                    8 * features // quarter, quarter
                ),
            ],
            axis=0,
        )

    small_sum = reduce_exact([slot_small(k) for k in range(4)])
    big = [reduce_slots(g) for g in (g_z, g_x, g_out)]
    gw_bc = jnp.sum(gw_bc.reshape(4, 8, 2 * LANES), axis=1) + gw_fix[:, inner:]
    common = jnp.concatenate(
        [
            g_bc,
            gw_bc,
            jnp.sum(gb_bc, axis=0)[None],
            jnp.sum(ggain_in, axis=0).reshape(3, 2 * LANES),
        ],
        axis=0,
    )
    big, small_sum, common = lax.psum((big, small_sum, lax.psum(common, "head")), "seq")
    gi = common[features + 5 :].reshape(features)
    gi = lax.dynamic_slice(gi, (hi_ * piece,), (piece,))
    row = small_sum[6]
    g_dt_own = small_sum[8:].reshape(8, features)[:heads].T
    return (
        layer_out,
        input_grad,
        gi,
        big[0],
        big[1],
        common[:features],
        g_dt_own,
        small_sum[0:4].T,
        small_sum[4],
        common[features : features + 4].T,
        common[features + 4],
        row[:heads],
        row[heads : 2 * heads],
        row[2 * heads : 3 * heads],
        small_sum[5],
        big[2],
    )


def solution(mesh):
    return jax.shard_map(
        shards,
        mesh=mesh,
        in_specs=(
            P(None, "seq", None),
            P(None, "seq", "head"),
            P(),
            P(None, "head"),
            P(None, "head"),
            P(),
            P(None, "head"),
            P("head", None),
            P("head"),
            P(),
            P(),
            P("head"),
            P("head"),
            P("head"),
            P("head"),
            P("head", None),
            P(),
        ),
        out_specs=(
            P(None, "seq", "head"),
            P(None, "seq", "head"),
            P("head"),
            P(None, "head"),
            P(None, "head"),
            P(),
            P(None, "head"),
            P("head", None),
            P("head"),
            P(),
            P(),
            P("head"),
            P("head"),
            P("head"),
            P("head"),
            P("head", None),
        ),
        check_vma=False,
    )
```

time: 996 us -> 654 us (0.66)
  other arithmetic: 234 us -> 24.6 us
  local copies, waits for them, and re-layouts: 246 us -> 63.1 us
  Pallas kernels: 0 us -> 163 us
  matrix products: 197 us -> 35.2 us
  starting transfers between devices: 7.91 us -> 50 us
  waiting for transfers between devices: 171 us -> 185 us
    pallas_call x0 -> x14, Pallas kernels: none -> 163 us  [the longest x12 160 us: run(): pl.pallas_call(kernel, grid_spec=pltpu.PrefetchScalarGridSpec(num_scalar_...]
    dot_general x27 -> x15, matrix products: 197 us -> 35.2 us  [token_dot(): lax.dot_general(a, b, (((0,), (0,)), ((), ())), preferred_element_type=f32)]
    scatter-add x4 -> x0, local copies, waits for them, and re-layouts: 124 us -> none  [the longest x3 118 us: shards(): d_pad.at[:, tap_index:tap_index + tokens]]
    ppermute x2 -> x30, waiting for transfers between devices: 0.01 us -> 64.7 us  [the longest x8 62.4 us: cross(): return lax.ppermute(x, 'head', across)]
    reduce_sum x10 -> x18, other arithmetic: 63.2 us -> 5.71 us  [the longest x4 2.52 us: slot_small(): jnp.sum(jnp.sum(gskip, axis=0)[k * quarter:(k + 1) * quarter].reshape(hea...]
    reduce_scatter x2 -> x0, waiting for transfers between devices: 50.8 us -> none  [the longest x1 50.8 us: shards(): lax.psum_scatter(partial_in, 'head', scatter_dimension=2, tiled=True)]
    add x8, other arithmetic: 39.7 us -> 1.68 us  [the longest x2 1.6 us: exchange(): chip_s = follow_k * lead_s + follow_s]
    convert_element_type x5 -> x0, other arithmetic: 36.6 us -> none  [the longest x1 13.2 us: shards(): activ = jax.nn.silu(conv_out).astype(jnp.bfloat16)]
  transfers between devices with their start and end apart: 9 -> 39, of which waited for: 3 -> 12; matrix products, arithmetic and copies ran while one was open for 53% -> 15% of each run, Pallas kernels for 0% -> 13%
where the time goes in v1:
time: 654 us; the launch traced here: 643 us
  waiting for transfers between devices  185 us (28%)
  Pallas kernels  163 us (25%)
  blocking collectives  106 us (16%)
  local copies, waits for them, and re-layouts  63.1 us (10%)
  starting transfers between devices  50 us (8%)
  matrix products  35.2 us (5%)
  other arithmetic  24.6 us (4%)
  between operations  15.7 us (2%)
    pallas_call x12, Pallas kernels, run(): pl.pallas_call(kernel, grid_spec=pltpu.PrefetchScalarGridSpec(num_scalar_...  160 us
    psum x1, waiting for transfers between devices, shards(): lax.psum((big, small_sum, lax.psum(common, 'head')), 'seq')  91 us
    all_gather x2, blocking collectives, exchange(): keeps = lax.all_gather(chip_k, 'seq', axis=0)  66.3 us
    ppermute x8, waiting for transfers between devices, cross(): return lax.ppermute(x, 'head', across)  62.4 us
    psum x1, blocking collectives, shards(): lax.psum((big, small_sum, lax.psum(common, 'head')), 'seq')  39.8 us
    dot_general x15, matrix products, token_dot(): lax.dot_general(a, b, (((0,), (0,)), ((), ())), preferred_element_type=f32)  35.2 us
    unnamed x144, local copies, waits for them, and re-layouts  17.7 us
    psum x1, waiting for transfers between devices, shards(): lax.psum(common, 'head')  14.7 us
  transfers between devices with their start and end apart: 39, of which 12 were waited for; matrix products, arithmetic and copies ran while one was open for 15% of the time, Pallas kernels for 13%

profile of v1, /device:TPU:0, one launch (start us, length us, event | category | flops | bytes accessed | tf_op | source)
XLA Modules:
  0.0 643.2 jit_solution(6318956926408382907)
XLA Ops:
  11.3 2.6 collective-permute-start.8
  14.8 3.8 collective-permute-start
  22.2 3.0 copy.51
  31.1 6.1 shard_map.315
  46.7 11.8 %shard_map.316 = (bf16[1024,768]{1,0:T(8,128)(2,1)}, f32[1024,768]{1,0:T(8,128)}, bf16[1024,768]{1,0:T(8,128)(2,1)}, f32[1024,128]{1,0:T(8,128)}, f32[1024,128]{...) custom-call(bf16[1024,768]{1,0:T(8,128)(2,1)} %get-tuple-element.95., ...), custom_call_target="tpu_custom_call" | custom-call | flops 6442450944 | bytes 16000000 | tf_op jit(solution)/shard_map/pallas_call | solution.py:81
  59.3 11.8 %shard_map.318 = (bf16[1024,768]{1,0:T(8,128)(2,1)}, f32[1024,768]{1,0:T(8,128)}, bf16[1024,768]{1,0:T(8,128)(2,1)}, f32[1024,128]{1,0:T(8,128)}, f32[1024,128]{...) custom-call(bf16[1024,768]{1,0:T(8,128)(2,1)} %get-tuple-element.95., ...), custom_call_target="tpu_custom_call" | custom-call | flops 6442450944 | bytes 16000000 | tf_op jit(solution)/shard_map/pallas_call | solution.py:81
  75.0 4.9 all-to-all-start.1
  83.1 33.9 %all-gather.2.keep = f32[8,1,768]{2,1,0:T(1,128)} all-gather(f32[1,1,768]{2,1,0:T(1,128)S(1)} %get-tuple-element.246), channel_id=2, replica_groups=mesh['seq'=8,'head'=4] {'seq'}, dimensions={0}, use_global_device_ids=true | all-gather | bytes 27648 | tf_op jit(solution)/shard_map/all_gather | solution.py:804
  119.6 3.5 all-to-all-start.2
  123.1 6.3 shard_map.317.part_a
  129.3 2.9 all-to-all-done.2
  132.2 4.0 all-to-all-start
  136.9 6.2 shard_map.319.part_b
  144.4 11.9 %all-to-all-done = bf16[4,1024,192]{1,2,0:T(8,128)(2,1)S(1)} async-done(((bf16[4,1024,192]{1,2,0:T(8,128)(2,1)}), bf16[4,1024,192]{1,2,0:T(8,128)(2,1)S(1)}, u32[]{:S(2)}, u32[]{:S(2)}) %all-to-all-start) | async-done | bytes 1572896 | tf_op jit(solution)/shard_map/all_to_all | solution.py:650
  156.3 2.5 copy.53.cot
  160.4 40.9 %shard_map.321 = (bf16[4,1024,192]{2,1,0:T(8,128)(2,1)}, bf16[1024,1536]{1,0:T(8,128)(2,1)}, bf16[1024,768]{1,0:T(8,128)(2,1)}, bf16[1024,1536]{1,0:T(8,128)(2,1...) custom-call(s32[2]{0:T(128)} %pad_add_fusion.meta, ...), custom_call_target="tpu_custom_call" | custom-call | flops 30000001024 | bytes 50000000 | tf_op jit(solution)/shard_map/pallas_call | solution.py:81
  204.2 11.1 %shard_map.322 = (f32[1024,768]{1,0:T(8,128)}, f32[1024,128]{1,0:T(8,128)}, f32[1024,128]{1,0:T(8,128)}, f32[1024,128]{1,0:T(8,128)}, f32[1024,128]{1,0:T(8,128)}) custom-call(bf16[1024,768]{1,0:T(8,128)(2,1)} %get-tuple-element.99.val.val_a, bf16[1024,1536]{1,0:T(8,128)(2,1)} %get-tuple-element.118.dssd, bf16[1024,128]{1,0:T(8,128)(2,1)} %get-tuple-element.98.bmat, ...), custom_call_target="tpu_custom_call" | custom-call | flops 15000000512 | bytes 10000000 | tf_op jit(solution)/shard_map/pallas_call | solution.py:81
  215.3 11.2 %shard_map.325 = (f32[1024,768]{1,0:T(8,128)}, f32[1024,128]{1,0:T(8,128)}, f32[1024,128]{1,0:T(8,128)}, f32[1024,128]{1,0:T(8,128)}, f32[1024,128]{1,0:T(8,128)}) custom-call(bf16[1024,768]{1,0:T(8,128)(2,1)} %get-tuple-element.102.val.val_b, bf16[1024,1536]{1,0:T(8,128)(2,1)} %get-tuple-element.118.dssd, bf16[1024,128]{1,0:T(8,128)(2,1)} %get-tuple-element.98.bmat, ...), custom_call_target="tpu_custom_call" | custom-call | flops 15000000512 | bytes 10000000 | tf_op jit(solution)/shard_map/pallas_call | solution.py:81
  226.6 3.0 convolution_convert_fusion.4
  231.7 3.6 all-to-all-start.4
  235.3 3.0 convolution_convert_fusion.5
  238.3 3.3 convolution_convert_fusion
  241.6 32.3 %all-gather.3.keep = f32[8,1,768]{2,1,0:T(1,128)} all-gather(f32[1,1,768]{2,1,0:T(1,128)S(1)} %get-tuple-element.243), channel_id=3, replica_groups=mesh['seq'=8,'head'=4] {'seq'}, dimensions={0}, use_global_device_ids=true | all-gather | bytes 27648 | tf_op jit(solution)/shard_map/all_gather | solution.py:804
  276.5 5.1 all-to-all-start.5
  287.1 3.1 fusion.3
  290.7 2.8 convolution_convert_fusion.1
  293.5 3.9 copy.54
  297.3 3.6 all-to-all-start.3
  301.0 2.6 fusion.5
  303.6 2.0 collective-permute-start.29
  306.8 3.5 fusion.2
  311.3 23.9 %collective-permute-done.29 = bf16[384,768]{1,0:T(8,128)(2,1)S(1)} collective-permute-done((bf16[384,768]{1,0:T(8,128)(2,1)S(1)}, bf16[384,768]{1,0:T(8,128)(2,1)S(1)}, u32[]{:S(2)}, u32[]{:S(2)}) %collective-permute-start.29) | collective-permute-done | bytes 589856 | tf_op jit(solution)/shard_map/ppermute | solution.py:621
  335.2 3.2 fusion
  343.5 17.1 %shard_map.324 = (bf16[1024,768]{1,0:T(8,128)(2,1)}, f32[8,768]{1,0:T(8,128)}, f32[8,768]{1,0:T(8,128)}, f32[1024,128]{1,0:T(8,128)}, bf16[1024,128]{1,0:T(8,128...) custom-call(bf16[1024,768]{1,0:T(8,128)(2,1)} %get-tuple-element.99.val.val_a, ...), custom_call_target="tpu_custom_call" | custom-call | flops 15000000512 | bytes 20000000 | tf_op jit(solution)/shard_map/pallas_call | solution.py:81
  363.5 17.1 %shard_map.326 = (bf16[1024,768]{1,0:T(8,128)(2,1)}, f32[8,768]{1,0:T(8,128)}, f32[8,768]{1,0:T(8,128)}, f32[1024,128]{1,0:T(8,128)}, bf16[1024,128]{1,0:T(8,128...) custom-call(bf16[1024,768]{1,0:T(8,128)(2,1)} %get-tuple-element.102.val.val_b, ...), custom_call_target="tpu_custom_call" | custom-call | flops 15000000512 | bytes 20000000 | tf_op jit(solution)/shard_map/pallas_call | solution.py:81
  382.2 5.1 shard_map.327
  392.7 2.3 convolution_convert_fusion.2
  395.0 2.8 collective-permute-start.22
  400.3 15.1 %shard_map.328 = (bf16[4,1024,192]{2,1,0:T(8,128)(2,1)}, f32[8,768]{1,0:T(8,128)}) custom-call(s32[2]{0:T(128)} %pad_add_fusion.meta, bf16[2,2048,768]{2,1,0:T(8,128)(2,1)} %hid.5, bf16[1024,768]{1,0:T(8,128)(2,1)} %get-tuple-element.116.cotx, f32[1,768]{1,0:T(1,128)} %broadcast_in_dim.152.gain, bf16[1024,1536]{1,0:T(8,128)(2,1)} %get-tuple-element.117.dgate, ...), custom_call_target="tpu_custom_call" | custom-call | flops 12000000000 | bytes 20000000 | tf_op jit(solution)/shard_map/pallas_call | solution.py:81
  419.6 20.0 %collective-permute-done.23 = bf16[768,384]{1,0:T(8,128)(2,1)} collective-permute-done((bf16[768,384]{1,0:T(8,128)(2,1)}, bf16[768,384]{1,0:T(8,128)(2,1)}, u32[]{:S(2)}, u32[]{:S(2)}) %collective-permute-start.23) | collective-permute-done | bytes 589856 | tf_op jit(solution)/shard_map/ppermute | solution.py:621
  439.6 3.4 fusion.1
  442.9 14.7 %all-reduce.23.cloned.1.call-done = f32[776,256]{1,0:T(8,128)} async-done(((f32[776,256]{1,0:T(8,128)}), f32[776,256]{1,0:T(8,128)}) %all-reduce.23.cloned.1.call-update) | async-done | bytes 794640 | tf_op jit(solution)/shard_map/psum | solution.py:1126
  460.3 3.9 copy.56
  464.2 3.7 all-to-all-start.6
  471.5 17.3 %collective-permute-done.26 = f32[24,384]{1,0:T(8,128)S(1)} collective-permute-done((f32[24,384]{1,0:T(8,128)S(1)}, f32[24,384]{1,0:T(8,128)S(1)}, u32[]{:S(2)}, u32[]{:S(2)}) %collective-permute-start.26) | collective-permute-done | bytes 36896 | tf_op jit(solution)/shard_map/ppermute | solution.py:621
  488.8 39.8 %psum.46 = f32[24,384]{1,0:T(8,128)S(1)} all-reduce(f32[24,384]{1,0:T(8,128)S(1)} %add_add_fusion), channel_id=1, replica_groups=mesh['seq'=8,'head'=4] {'seq'}, use_global_device_ids=true, to_apply=%region_26.27 | all-reduce | flops 9216 | bytes 73728 | tf_op jit(solution)/shard_map/psum | solution.py:1126
  535.0 91.0 %all-reduce.25.cloned.1.call-done = (f32[776,256]{1,0:T(8,128)}, f32[768,384]{1,0:T(8,128)}, f32[768,384]{1,0:T(8,128)}, f32[384,768]{1,0:T(8,128)}) async-done(((f32[776,256]{1,0:T(8,128)}, f32[768,384]{1,0:T(8,128)}, f32[768,384]{1,0:T(8,128)}, f32[384,768]{1,0:T(8,128)}), (f32[776,256]{1,0:T(8,128)}, f32[768,384]{1,0:T(8,128)}, f32[768,384]{1,0:T(8,128)}, ...) | async-done | bytes 4333584 | tf_op jit(solution)/shard_map/psum | solution.py:1126
  626.1 2.2 slice.658
  (388 shorter events, 95.1 us)
Async XLA Ops:
  7.2 12.2 %copy-start = (s32[2,84]{1,0:T(2,128)S(1)}, s32[2,84]{1,0:T(2,128)}, u32[]{:S(2)}) copy-start(s32[2,84]{1,0:T(2,128)} %param.36) | copy-start | bytes 2020
  10.8 27.7 %collective-permute-start.7 = (f32[24,384]{1,0:T(8,128)S(1)}, f32[24,384]{1,0:T(8,128)S(1)}, u32[]{:S(2)}, u32[]{:S(2)}) collective-permute-start(f32[24,384]{1,0:T(8,128)S(1)} %concatenate.145), channel_id=1, source_target_pairs={{0,1},{1,0},{2,3},{3,2},{4,5},{5,4},{6,7},{7,6},{8,9},{9,8},{10,11... | collective-permute-start | bytes 110600 | tf_op jit(solution)/shard_map/ppermute | solution.py:618
  11.3 29.8 %collective-permute-start.8 = (f32[24,384]{1,0:T(8,128)S(1)}, f32[24,384]{1,0:T(8,128)S(1)}, u32[]{:S(2)}, u32[]{:S(2)}) collective-permute-start(f32[24,384]{1,0:T(8,128)S(1)} %concatenate.145), channel_id=1, source_target_pairs={{0,2},{1,3},{2,0},{3,1},{4,6},{5,7},{6,4},{7,5},{8,10},{9,11},{10,... | collective-permute-start | bytes 110600 | tf_op jit(solution)/shard_map/ppermute | solution.py:621
  13.9 32.3 %collective-permute-start.11 = (bf16[768,384]{1,0:T(8,128)(2,1)}, bf16[768,384]{1,0:T(8,128)(2,1)}, u32[]{:S(2)}, u32[]{:S(2)}) collective-permute-start(bf16[768,384]{1,0:T(8,128)(2,1)} %x0.1), channel_id=1, source_target_pairs={{0,2},{1,3},{2,0},{3,1},{4,6},{5,7},{6,4},{7,5},{8,10},{9,11},{10,... | collective-permute-start | bytes 1769480 | tf_op jit(solution)/shard_map/ppermute | solution.py:621
  14.0 32.3 %collective-permute-start.10 = (bf16[768,384]{1,0:T(8,128)(2,1)}, bf16[768,384]{1,0:T(8,128)(2,1)}, u32[]{:S(2)}, u32[]{:S(2)}) collective-permute-start(bf16[768,384]{1,0:T(8,128)(2,1)} %x0.1), channel_id=1, source_target_pairs={{0,1},{1,0},{2,3},{3,2},{4,5},{5,4},{6,7},{7,6},{8,9},{9,8},{10,11... | collective-permute-start | bytes 1769480 | tf_op jit(solution)/shard_map/ppermute | solution.py:618
  14.8 12.5 %collective-permute-start = (bf16[16,768]{1,0:T(8,128)(2,1)S(1)}, bf16[16,768]{1,0:T(8,128)(2,1)S(1)}, u32[]{:S(2)}, u32[]{:S(2)}) collective-permute-start(bf16[16,768]{1,0:T(8,128)(2,1)S(1)} %dynamic-slice_bitcast_fusion), channel_id=1, source_target_pairs={{0,4},{4,8},{8,12},{12,16},{16,20},{20,24},{24,28},{1,5},{5,9},{9,... | collective-permute-start | bytes 73736 | tf_op jit(solution)/shard_map/ppermute | solution.py:639
  19.3 21.2 %copy-start.49 = (f32[6]{0:T(128)}, f32[6]{0:T(128)S(1)}, u32[]{:S(2)}) copy-start(f32[6]{0:T(128)S(1)} %get-tuple-element.331) | copy-start | bytes 76
  27.3 55.4 %collective-permute-start.2 = (bf16[768,384]{1,0:T(8,128)(2,1)}, bf16[768,384]{1,0:T(8,128)(2,1)}, u32[]{:S(2)}, u32[]{:S(2)}) collective-permute-start(bf16[768,384]{1,0:T(8,128)(2,1)} %z0.3), channel_id=1, source_target_pairs={{0,2},{1,3},{2,0},{3,1},{4,6},{5,7},{6,4},{7,5},{8,10},{9,11},{10,... | collective-permute-start | bytes 1769480 | tf_op jit(solution)/shard_map/ppermute | solution.py:621
  38.5 121.9 %collective-permute-start.1 = (bf16[768,384]{1,0:T(8,128)(2,1)}, bf16[768,384]{1,0:T(8,128)(2,1)}, u32[]{:S(2)}, u32[]{:S(2)}) collective-permute-start(bf16[768,384]{1,0:T(8,128)(2,1)} %z0.3), channel_id=1, source_target_pairs={{0,1},{1,0},{2,3},{3,2},{4,5},{5,4},{6,7},{7,6},{8,9},{9,8},{10,11... | collective-permute-start | bytes 1769480 | tf_op jit(solution)/shard_map/ppermute | solution.py:618
  40.5 18.0 %copy-start.55 = (f32[6]{0:T(128)}, f32[6]{0:T(128)S(1)}, u32[]{:S(2)}) copy-start(f32[6]{0:T(128)S(1)} %get-tuple-element.285) | copy-start | bytes 76
  41.1 1.4 collective-permute-start.9
  42.5 40.2 %collective-permute-start.5 = (bf16[384,768]{1,0:T(8,128)(2,1)}, bf16[384,768]{1,0:T(8,128)(2,1)}, u32[]{:S(2)}, u32[]{:S(2)}) collective-permute-start(bf16[384,768]{1,0:T(8,128)(2,1)} %o0.1), channel_id=1, source_target_pairs={{0,2},{1,3},{2,0},{3,1},{4,6},{5,7},{6,4},{7,5},{8,10},{9,11},{10,... | collective-permute-start | bytes 1769480 | tf_op jit(solution)/shard_map/ppermute | solution.py:621
  46.2 114.2 %collective-permute-start.4 = (bf16[384,768]{1,0:T(8,128)(2,1)}, bf16[384,768]{1,0:T(8,128)(2,1)}, u32[]{:S(2)}, u32[]{:S(2)}) collective-permute-start(bf16[384,768]{1,0:T(8,128)(2,1)} %o0.1), channel_id=1, source_target_pairs={{0,1},{1,0},{2,3},{3,2},{4,5},{5,4},{6,7},{7,6},{8,9},{9,8},{10,11... | collective-permute-start | bytes 1769480 | tf_op jit(solution)/shard_map/ppermute | solution.py:618
  46.3 12.2 %collective-permute-start.12 = (bf16[768,384]{1,0:T(8,128)(2,1)}, bf16[768,384]{1,0:T(8,128)(2,1)S(1)}, u32[]{:S(2)}, u32[]{:S(2)}) collective-permute-start(bf16[768,384]{1,0:T(8,128)(2,1)} %collective-permute-done.11.wa.x2), channel_id=1, source_target_pairs={{0,1},{1,0},{2,3},{3,2},{4,5},{5,4},{6,7},{7,6},{8,9},{9,8},{10,11... | collective-permute-start | bytes 1769480 | tf_op jit(solution)/shard_map/ppermute | solution.py:618
  58.5 12.6 %copy-start.12 = (f32[128,768]{1,0:T(8,128)S(1)}, f32[128,768]{1,0:T(8,128)}, u32[]{:S(2)}) copy-start(f32[128,768]{1,0:T(8,128)} %get-tuple-element.111) | copy-start | bytes 1179652
  72.3 1.8 collective-permute-start.13
  75.0 42.0 %all-to-all-start.1 = ((f32[8,16,768]{2,1,0:T(8,128)}), f32[8,16,768]{2,1,0:T(8,128)S(1)}, u32[]{:S(2)}, u32[]{:S(2)}) async-start(f32[8,16,768]{2,1,0:T(8,128)} %bitcast.30), calls=%async_computation.1 | async-start | bytes 786432 | tf_op jit(solution)/shard_map/all_to_all | solution.py:805
  82.6 77.8 %collective-permute-start.3 = (bf16[768,384]{1,0:T(8,128)(2,1)}, bf16[768,384]{1,0:T(8,128)(2,1)}, u32[]{:S(2)}, u32[]{:S(2)}) collective-permute-start(bf16[768,384]{1,0:T(8,128)(2,1)} %collective-permute-done.2.z2), channel_id=1, source_target_pairs={{0,1},{1,0},{2,3},{3,2},{4,5},{5,4},{6,7},{7,6},{8,9},{9,8},{10,11... | collective-permute-start | bytes 1769480 | tf_op jit(solution)/shard_map/ppermute | solution.py:618
  82.6 77.8 %collective-permute-start.6 = (bf16[384,768]{1,0:T(8,128)(2,1)}, bf16[384,768]{1,0:T(8,128)(2,1)}, u32[]{:S(2)}, u32[]{:S(2)}) collective-permute-start(bf16[384,768]{1,0:T(8,128)(2,1)} %collective-permute-done.5.o2), channel_id=1, source_target_pairs={{0,1},{1,0},{2,3},{3,2},{4,5},{5,4},{6,7},{7,6},{8,9},{9,8},{10,11... | collective-permute-start | bytes 1769480 | tf_op jit(solution)/shard_map/ppermute | solution.py:618
  119.6 12.6 %all-to-all-start.2 = ((f32[8,16,768]{2,1,0:T(8,128)}), f32[8,16,768]{2,1,0:T(8,128)S(1)}, u32[]{:S(2)}, u32[]{:S(2)}) async-start(f32[8,16,768]{2,1,0:T(8,128)} %shard_map.320), calls=%async_computation.2 | async-start | bytes 786432 | tf_op jit(solution)/shard_map/all_to_all | solution.py:810
  132.2 24.1 %all-to-all-start = ((bf16[4,1024,192]{1,2,0:T(8,128)(2,1)}), bf16[4,1024,192]{1,2,0:T(8,128)(2,1)S(1)}, u32[]{:S(2)}, u32[]{:S(2)}) async-start(bf16[4,1024,192]{1,2,0:T(8,128)(2,1)} %copy.52), calls=%async_computation | async-start | bytes 3145728 | tf_op jit(solution)/shard_map/all_to_all | solution.py:650
  136.3 22.5 %collective-permute-start.14 = (f32[128,768]{1,0:T(8,128)S(1)}, f32[128,768]{1,0:T(8,128)S(1)}, u32[]{:S(2)}, u32[]{:S(2)}) collective-permute-start(f32[128,768]{1,0:T(8,128)S(1)} %get-tuple-element.241), channel_id=1, source_target_pairs={{0,1},{1,0},{2,3},{3,2},{4,5},{5,4},{6,7},{7,6},{8,9},{9,8},{10,11... | collective-permute-start | bytes 1179656 | tf_op jit(solution)/shard_map/ppermute | solution.py:618
  203.5 26.5 %collective-permute-start.15 = (f32[136,768]{1,0:T(8,128)S(1)}, f32[136,768]{1,0:T(8,128)S(1)}, u32[]{:S(2)}, u32[]{:S(2)}) collective-permute-start(f32[136,768]{1,0:T(8,128)S(1)} %maximum_maximum_fusion.2), channel_id=1, source_target_pairs={{0,1},{1,0},{2,3},{3,2},{4,5},{5,4},{6,7},{7,6},{8,9},{9,8},{10,11... | collective-permute-start | bytes 1253384 | tf_op jit(solution)/shard_map/ppermute | solution.py:618
  215.3 11.2 %copy-start.19 = (f32[8,1536]{1,0:T(8,128)S(1)}, f32[8,1536]{1,0:T(8,128)}, u32[]{:S(2)}) copy-start(f32[8,1536]{1,0:T(8,128)} %get-tuple-element.168) | copy-start | bytes 147460
  215.3 11.2 %copy-start.2 = (bf16[1024,768]{1,0:T(8,128)(2,1)S(1)}, bf16[1024,768]{1,0:T(8,128)(2,1)}, u32[]{:S(2)}) copy-start(bf16[1024,768]{1,0:T(8,128)(2,1)} %get-tuple-element.95.normed) | copy-start | bytes 4718596
  229.5 57.6 %collective-permute-start.19 = (bf16[768,384]{1,0:T(8,128)(2,1)}, bf16[768,384]{1,0:T(8,128)(2,1)}, u32[]{:S(2)}, u32[]{:S(2)}) collective-permute-start(bf16[768,384]{1,0:T(8,128)(2,1)} %convolution_convert_fusion.4), channel_id=1, source_target_pairs={{0,1},{1,0},{2,3},{3,2},{4,5},{5,4},{6,7},{7,6},{8,9},{9,8},{10,11... | collective-permute-start | bytes 1769480 | tf_op jit(solution)/shard_map/ppermute | solution.py:618
  231.7 42.3 %all-to-all-start.4 = ((f32[8,16,768]{2,1,0:T(8,128)}), f32[8,16,768]{2,1,0:T(8,128)S(1)}, u32[]{:S(2)}, u32[]{:S(2)}) async-start(f32[8,16,768]{2,1,0:T(8,128)} %bitcast.33), calls=%async_computation.4 | async-start | bytes 786432 | tf_op jit(solution)/shard_map/all_to_all | solution.py:805
  276.5 20.8 %all-to-all-start.5 = ((f32[8,16,768]{2,1,0:T(8,128)}), f32[8,16,768]{2,1,0:T(8,128)S(1)}, u32[]{:S(2)}, u32[]{:S(2)}) async-start(f32[8,16,768]{2,1,0:T(8,128)} %shard_map.323), calls=%async_computation.5 | async-start | bytes 786432 | tf_op jit(solution)/shard_map/all_to_all | solution.py:810
  286.6 14.3 %collective-permute-start.28 = (bf16[384,768]{1,0:T(8,128)(2,1)}, bf16[384,768]{1,0:T(8,128)(2,1)}, u32[]{:S(2)}, u32[]{:S(2)}) collective-permute-start(bf16[384,768]{1,0:T(8,128)(2,1)} %convolution_convert_fusion), channel_id=1, source_target_pairs={{0,1},{1,0},{2,3},{3,2},{4,5},{5,4},{6,7},{7,6},{8,9},{9,8},{10,11... | collective-permute-start | bytes 1769480 | tf_op jit(solution)/shard_map/ppermute | solution.py:618
  286.6 18.9 %collective-permute-start.18 = (bf16[768,384]{1,0:T(8,128)(2,1)}, bf16[768,384]{1,0:T(8,128)(2,1)}, u32[]{:S(2)}, u32[]{:S(2)}) collective-permute-start(bf16[768,384]{1,0:T(8,128)(2,1)} %convolution_convert_fusion.5), channel_id=1, source_target_pairs={{0,1},{1,0},{2,3},{3,2},{4,5},{5,4},{6,7},{7,6},{8,9},{9,8},{10,11... | collective-permute-start | bytes 1769480 | tf_op jit(solution)/shard_map/ppermute | solution.py:618
  290.3 16.5 %collective-permute-start.20 = (bf16[768,384]{1,0:T(8,128)(2,1)}, bf16[768,384]{1,0:T(8,128)(2,1)}, u32[]{:S(2)}, u32[]{:S(2)}) collective-permute-start(bf16[768,384]{1,0:T(8,128)(2,1)} %fusion.3), channel_id=1, source_target_pairs={{0,2},{1,3},{2,0},{3,1},{4,6},{5,7},{6,4},{7,5},{8,10},{9,11},{10,... | collective-permute-start | bytes 1769480 | tf_op jit(solution)/shard_map/ppermute | solution.py:621
  293.5 17.8 %collective-permute-start.27 = (bf16[384,768]{1,0:T(8,128)(2,1)}, bf16[384,768]{1,0:T(8,128)(2,1)}, u32[]{:S(2)}, u32[]{:S(2)}) collective-permute-start(bf16[384,768]{1,0:T(8,128)(2,1)} %convolution_convert_fusion.1), channel_id=1, source_target_pairs={{0,1},{1,0},{2,3},{3,2},{4,5},{5,4},{6,7},{7,6},{8,9},{9,8},{10,11... | collective-permute-start | bytes 1769480 | tf_op jit(solution)/shard_map/ppermute | solution.py:618
  297.3 41.1 %all-to-all-start.3 = ((bf16[4,1024,192]{1,2,0:T(8,128)(2,1)}), bf16[4,1024,192]{1,2,0:T(8,128)(2,1)S(1)}, u32[]{:S(2)}, u32[]{:S(2)}) async-start(bf16[4,1024,192]{1,2,0:T(8,128)(2,1)} %copy.54), calls=%async_computation.3 | async-start | bytes 3145728 | tf_op jit(solution)/shard_map/all_to_all | solution.py:883
  300.9 156.7 %all-reduce.23.cloned.1.call-start = ((), (), s32[]{:S(2)}) async-start(), calls=%async_computation.7 | async-start | bytes 1589248 | tf_op jit(solution)/shard_map/psum | solution.py:1126
  303.6 31.7 %collective-permute-start.29 = (bf16[384,768]{1,0:T(8,128)(2,1)S(1)}, bf16[384,768]{1,0:T(8,128)(2,1)S(1)}, u32[]{:S(2)}, u32[]{:S(2)}) collective-permute-start(bf16[384,768]{1,0:T(8,128)(2,1)S(1)} %fusion.5), channel_id=1, source_target_pairs={{0,2},{1,3},{2,0},{3,1},{4,6},{5,7},{6,4},{7,5},{8,10},{9,11},{10,... | collective-permute-start | bytes 1769480 | tf_op jit(solution)/shard_map/ppermute | solution.py:621
  310.3 24.9 %copy-start.64 = (bf16[1024,768]{1,0:T(8,128)(2,1)S(1)}, bf16[1024,768]{1,0:T(8,128)(2,1)}, u32[]{:S(2)}) copy-start(bf16[1024,768]{1,0:T(8,128)(2,1)} %get-tuple-element.116.cotx) | copy-start | bytes 4718596
  311.3 31.4 %collective-permute-start.16 = (f32[128,768]{1,0:T(8,128)}, f32[128,768]{1,0:T(8,128)S(1)}, u32[]{:S(2)}, u32[]{:S(2)}) collective-permute-start(f32[128,768]{1,0:T(8,128)} %get-tuple-element.239), channel_id=1, source_target_pairs={{0,1},{1,0},{2,3},{3,2},{4,5},{5,4},{6,7},{7,6},{8,9},{9,8},{10,11... | collective-permute-start | bytes 1179656 | tf_op jit(solution)/shard_map/ppermute | solution.py:618
  382.2 10.6 %copy-start.3 = (bf16[1024,768]{1,0:T(8,128)(2,1)S(1)}, bf16[1024,768]{1,0:T(8,128)(2,1)}, u32[]{:S(2)}) copy-start(bf16[1024,768]{1,0:T(8,128)(2,1)} %get-tuple-element.95.normed) | copy-start | bytes 4718596
  387.9 3.1 collective-permute-start.17
  395.0 20.4 %collective-permute-start.22 = (bf16[768,384]{1,0:T(8,128)(2,1)S(1)}, bf16[768,384]{1,0:T(8,128)(2,1)S(1)}, u32[]{:S(2)}, u32[]{:S(2)}) collective-permute-start(bf16[768,384]{1,0:T(8,128)(2,1)S(1)} %convolution_convert_fusion.2), channel_id=1, source_target_pairs={{0,1},{1,0},{2,3},{3,2},{4,5},{5,4},{6,7},{7,6},{8,9},{9,8},{10,11... | collective-permute-start | bytes 1769480 | tf_op jit(solution)/shard_map/ppermute | solution.py:618
  399.7 19.9 %collective-permute-start.21 = (bf16[768,384]{1,0:T(8,128)(2,1)}, bf16[768,384]{1,0:T(8,128)(2,1)S(1)}, u32[]{:S(2)}, u32[]{:S(2)}) collective-permute-start(bf16[768,384]{1,0:T(8,128)(2,1)} %convolution_convert_fusion.3), channel_id=1, source_target_pairs={{0,1},{1,0},{2,3},{3,2},{4,5},{5,4},{6,7},{7,6},{8,9},{9,8},{10,11... | collective-permute-start | bytes 1769480 | tf_op jit(solution)/shard_map/ppermute | solution.py:618
  400.3 15.2 %copy-start.60 = (bf16[1024,768]{1,0:T(8,128)(2,1)S(1)}, bf16[1024,768]{1,0:T(8,128)(2,1)}, u32[]{:S(2)}) copy-start(bf16[1024,768]{1,0:T(8,128)(2,1)} %get-tuple-element.291.dx_b) | copy-start | bytes 4718596
  417.3 22.3 %collective-permute-start.23 = (bf16[768,384]{1,0:T(8,128)(2,1)}, bf16[768,384]{1,0:T(8,128)(2,1)}, u32[]{:S(2)}, u32[]{:S(2)}) collective-permute-start(bf16[768,384]{1,0:T(8,128)(2,1)} %fusion.4), channel_id=1, source_target_pairs={{0,2},{1,3},{2,0},{3,1},{4,6},{5,7},{6,4},{7,5},{8,10},{9,11},{10,... | collective-permute-start | bytes 1769480 | tf_op jit(solution)/shard_map/ppermute | solution.py:621
  419.4 206.7 %all-reduce.25.cloned.1.call-start = ((), (), s32[]{:S(2)}) async-start(), calls=%async_computation.8 | async-start | bytes 8667136 | tf_op jit(solution)/shard_map/psum | solution.py:1126
  464.2 66.8 %all-to-all-start.6 = ((bf16[4,1024,192]{1,2,0:T(8,128)(2,1)}), bf16[4,1024,192]{1,2,0:T(8,128)(2,1)S(1)}, u32[]{:S(2)}, u32[]{:S(2)}) async-start(bf16[4,1024,192]{1,2,0:T(8,128)(2,1)} %copy.56), calls=%async_computation.6 | async-start | bytes 3145728 | tf_op jit(solution)/shard_map/all_to_all | solution.py:1063
  468.0 1.6 collective-permute-start.25
  468.6 2.9 collective-permute-start.24
  469.7 19.1 %collective-permute-start.26 = (f32[24,384]{1,0:T(8,128)S(1)}, f32[24,384]{1,0:T(8,128)S(1)}, u32[]{:S(2)}, u32[]{:S(2)}) collective-permute-start(f32[24,384]{1,0:T(8,128)S(1)} %add.190), channel_id=1, source_target_pairs={{0,2},{1,3},{2,0},{3,1},{4,6},{5,7},{6,4},{7,5},{8,10},{9,11},{10,... | collective-permute-start | bytes 110600 | tf_op jit(solution)/shard_map/ppermute | solution.py:621
  (56 other events, 213.7 us)
Sparse Core Ops, SparseCore 0:
  419.5 38.0 all-reduce.22
  462.8 163.2 all-reduce.24
